TPU v7x, 256 devices: a whole 4x4x8 slice. The times are simulated.
256 devices in a mesh: section: 8 (over z_lo, core), expert: 32 (over y, z_hi, x).
Axes of the slice: x: 4, y: 4, z: 8 (z_hi: 2, z_lo: 4; z = z_hi * 4 + z_lo), core: 2. Of those that a mesh axis runs over, the one named last changes fastest.
Arguments:
- x_held: bfloat16 [8, 4096, 2048], P('section', 'expert'), may hold values from -6 to 6
- grad_held: bfloat16 [8, 4096, 2048], P('section', 'expert'), may hold values from -6 to 6
- expert_ids: int32 [8, 4096, 4], P('section', 'expert'), may hold values from 0 to 27, all different within a row; in each aligned block of 128 rows (0 to 127, 128 to 255, ..., all dimensions but the last counted through in order) at most 23 rows name the same one
- gate_logits: float32 [8, 4096, 4], P('section', 'expert'), may hold values from -4 to 4
- placement: int32 [8, 32], P('section'), may hold values from 0 to 27, as said below
- w_gate_up: bfloat16 [8, 32, 2048, 1536], P('section', 'expert'), as said below
- w_down: bfloat16 [8, 32, 768, 2048], P('section', 'expert'), as said below
Outputs:
- section_out: bfloat16 [8, 4096, 2048], P('section', 'expert')
- input_grad: bfloat16 [8, 4096, 2048], P('section', 'expert')
- logit_grad: float32 [8, 4096, 4], P('section', 'expert')
Inputs may be any that keep to these rules, and one draw needn't show every extreme that they name: `expert_ids`: in each section and the 128 tokens of one device, no expert is named by more than 23 slots, a bound that some such block reaches; a token names 4 different experts. `placement`: in each section, copies 0 to 27 hold every expert once, and copies 28 to 31 hold 4 different experts, a second copy each. `w_gate_up`: two copies of one section that hold the same expert have equal weights. `w_down`: two copies of one section that hold the same expert have equal weights.
All inputs are finite; a program needn't handle non-finite values.
Results may differ from a plain program's by a relative error of at most 0.0064.
Values may be sent and summed in bfloat16 or wider, within the bound.
No kernel may reach another device: no remote copies, remote signals or barrier semaphores. Data moves between devices by JAX's collectives and lax.ppermute only.
A program may use at most 128 MiB of HBM per device.

v0:
```python
import jax
import jax.numpy as jnp
from jax import lax
from jax.sharding import PartitionSpec as P


def passed_along(x, axis, by):
    devices = lax.axis_size(axis)
    pairs = [(i, i + by) for i in range(devices) if 0 <= i + by < devices]
    return lax.ppermute(x, axis, pairs)


def routing(expert_list, table, experts):
    copies = table.shape[0]
    flat_ids = expert_list.reshape(-1)
    labels = jnp.arange(experts, dtype=jnp.int32)
    onehot = (flat_ids[:, None] == labels[None, :]).astype(jnp.int32)
    before = jnp.cumsum(onehot, axis=0) - onehot
    ranking = jnp.sum(before * onehot, axis=1)
    holding = (table[:, None] == labels[None, :]).astype(jnp.int32)
    number = jnp.arange(copies, dtype=jnp.int32)[:, None]
    first_mask = (number < experts).astype(jnp.int32)
    primary = jnp.sum(number * holding * first_mask, axis=0)
    second = jnp.sum(number * holding * (1 - first_mask), axis=0)
    doubled = jnp.sum(holding * (1 - first_mask), axis=0)
    to_first = jnp.sum(onehot * primary[None, :], axis=1)
    to_second = jnp.sum(onehot * second[None, :], axis=1)
    is_hot = jnp.sum(onehot * doubled[None, :], axis=1)
    target = jnp.where((is_hot > 0) & (ranking % 2 == 1), to_second, to_first)
    marked = (target[:, None] == jnp.arange(copies, dtype=jnp.int32)[None, :]).astype(jnp.int32)
    places = jnp.sum((jnp.cumsum(marked, axis=0) - marked) * marked, axis=1)
    return (target, places)


def slot_index(target, places, copies, capacity):
    total = target.shape[0]
    empty = jnp.full((copies * capacity,), total, dtype=jnp.int32)
    return empty.at[target * capacity + places].set(jnp.arange(total, dtype=jnp.int32))


def pick_rows(source, index):
    padded = jnp.concatenate([source, jnp.zeros((1, source.shape[1]), source.dtype)], axis=0)
    return jnp.take(padded, index, axis=0)


def expert_forward(rows, w_gu, w_dn, hidden_units):
    flat_rows = rows.reshape(-1, rows.shape[-1])
    pre_acts = jnp.dot(flat_rows, w_gu, preferred_element_type=jnp.float32)
    gate_pre = pre_acts[:, :hidden_units]
    up_pre = pre_acts[:, hidden_units:]
    hidden = (gate_pre * jax.nn.sigmoid(gate_pre) * up_pre).astype(jnp.bfloat16)
    produced = jnp.dot(hidden, w_dn, preferred_element_type=jnp.float32).astype(jnp.bfloat16)
    return (produced.reshape(rows.shape), pre_acts.reshape(rows.shape[:-1] + (pre_acts.shape[-1],)))


def expert_backward(grads, pre_acts, w_gu, w_dn, hidden_units):
    flat_grads = grads.reshape(-1, grads.shape[-1])
    flat_pre = pre_acts.reshape(-1, pre_acts.shape[-1])
    hidden_grad = lax.dot_general(
        flat_grads, w_dn, (((1,), (1,)), ((), ())), preferred_element_type=jnp.float32
    )
    gate_pre = flat_pre[:, :hidden_units]
    up_pre = flat_pre[:, hidden_units:]
    sigmoid_gate = jax.nn.sigmoid(gate_pre)
    pre_grad = jnp.concatenate(
        [
            hidden_grad * up_pre * sigmoid_gate * (1.0 + gate_pre * (1.0 - sigmoid_gate)),
            hidden_grad * gate_pre * sigmoid_gate,
        ],
        axis=1,
    ).astype(jnp.bfloat16)
    row_grad = lax.dot_general(
        pre_grad, w_gu, (((1,), (1,)), ((), ())), preferred_element_type=jnp.float32
    ).astype(jnp.bfloat16)
    return row_grad.reshape(grads.shape)


def local(x_held, grad_held, expert_ids, gate_logits, placement, w_gate_up, w_down):
    own_rows = x_held[0]
    own_grad = grad_held[0]
    section_pos = lax.axis_index("section")
    section_count = lax.axis_size("section")
    arrived = passed_along(own_rows, "section", 1)
    inputs = jnp.where(section_pos == 0, own_rows, arrived)
    later = passed_along(own_grad, "section", -1)
    upstream = jnp.where(section_pos == section_count - 1, own_grad, later)
    tok_count, width = inputs.shape
    topk = expert_ids.shape[2]
    hidden_units = w_down.shape[2]
    table = placement[0]
    copies = table.shape[0]
    experts = copies - copies // 8
    capacity = (5 * tok_count * topk + 4 * experts - 1) // (4 * experts)
    w_gu = w_gate_up[0, 0]
    w_dn = w_down[0, 0]
    raised = jnp.exp(gate_logits[0])
    gate_probs = raised / jnp.sum(raised, axis=1, keepdims=True)
    target, places = routing(expert_ids[0], table, experts)
    total = tok_count * topk
    index = slot_index(target, places, copies, capacity)
    token_of = jnp.where(index < total, index // topk, tok_count)
    outgoing = pick_rows(inputs, token_of).reshape(copies, capacity, width)
    scaled = (gate_probs[:, :, None] * upstream[:, None, :].astype(jnp.float32)).astype(
        jnp.bfloat16
    )
    grad_rows = pick_rows(scaled.reshape(total, width), index).reshape(copies, capacity, width)
    produced, pre_acts = expert_forward(
        lax.all_to_all(outgoing, "expert", split_axis=0, concat_axis=0, tiled=True),
        w_gu,
        w_dn,
        hidden_units,
    )
    returned = lax.all_to_all(produced, "expert", split_axis=0, concat_axis=0, tiled=True)
    grads_in = lax.all_to_all(grad_rows, "expert", split_axis=0, concat_axis=0, tiled=True)
    row_grad = expert_backward(grads_in, pre_acts, w_gu, w_dn, hidden_units)
    row_back = lax.all_to_all(row_grad, "expert", split_axis=0, concat_axis=0, tiled=True)
    where_from = target * capacity + places
    out_slots = jnp.take(returned.reshape(copies * capacity, width), where_from, axis=0).reshape(
        tok_count, topk, width
    )
    grad_slots = jnp.take(row_back.reshape(copies * capacity, width), where_from, axis=0).reshape(
        tok_count, topk, width
    )
    section_out = jnp.sum(gate_probs[:, :, None] * out_slots.astype(jnp.float32), axis=1).astype(
        jnp.bfloat16
    )
    gate_grad = jnp.einsum("tkd,td->tk", out_slots, upstream, preferred_element_type=jnp.float32)
    logit_grad = gate_probs * (gate_grad - jnp.sum(gate_probs * gate_grad, axis=1, keepdims=True))
    input_grad = jnp.sum(grad_slots.astype(jnp.float32), axis=1).astype(jnp.bfloat16)
    return (section_out[None], input_grad[None], logit_grad[None])


def solution(mesh):
    placed = (
        P("section", "expert", None),
        P("section", "expert", None),
        P("section", "expert", None),
        P("section", "expert", None),
        P("section", None),
        P("section", "expert", None, None),
        P("section", "expert", None, None),
    )
    return jax.shard_map(
        local,
        mesh=mesh,
        in_specs=placed,
        out_specs=(
            P("section", "expert", None),
            P("section", "expert", None),
            P("section", "expert", None),
        ),
        check_vma=False,
    )
```

profile of v0, /device:TPU:96, one launch (start us, length us, event | category | flops | bytes accessed | tf_op | source)
XLA Modules:
  0.0 419.5 jit_solution(12280521621589361478)
XLA Ops:
  13.8 8.2 %gather_fusion = bf16[736,2048]{1,0:T(8,128)(2,1)} fusion(bf16[129,2048]{1,0:T(8,128)(2,1)} %concatenate.10, s32[1024]{0:T(1024)S(1)} %pad_clamp_fusion.2), kind=kCustom, calls=%fused_computation.2 | custom fusion | bytes 6032256 | tf_op jit(solution)/shard_map/jit(_take)/gather | solution.py:43
  22.0 4.5 %gather.16 = bf16[32,23,2048]{2,1,0:T(8,128)(2,1)} reshape(bf16[736,2048]{1,0:T(8,128)(2,1)} %gather_fusion) | data formatting | bytes 6029312 | tf_op jit(solution)/shard_map/jit(_take)/gather | solution.py:43
  30.5 11.5 %all-to-all-start = ((bf16[32,23,2048]{2,1,0:T(8,128)(2,1)}), bf16[32,23,2048]{2,1,0:T(8,128)(2,1)}, u32[]{:S(2)}, u32[]{:S(2)}) async-start(bf16[32,23,2048]{2,1,0:T(8,128)(2,1)} %broadcast_select_fusion.1), calls=%async_computation | async-start | bytes 6291456 | tf_op jit(solution)/shard_map/all_to_all | solution.py:108
  44.8 52.1 %collective-permute-done.1 = bf16[128,2048]{1,0:T(8,128)(2,1)} collective-permute-done((bf16[128,2048]{1,0:T(8,128)(2,1)}, bf16[128,2048]{1,0:T(8,128)(2,1)}, u32[]{:S(2)}, u32[]{:S(2)}) %collective-permute-start.1) | collective-permute-done | bytes 524320 | tf_op jit(solution)/shard_map/ppermute | solution.py:10
  102.2 5.3 %mul.156 = f32[512,2048]{1,0:T(8,128)} reshape(f32[128,4,2048]{2,1,0:T(4,128)} %mul.155) | data formatting | bytes 8388608 | tf_op jit(solution)/shard_map/mul | solution.py:103
  111.5 8.9 %gather_fusion.1 = bf16[736,2048]{1,0:T(8,128)(2,1)} fusion(bf16[513,2048]{1,0:T(8,128)(2,1)} %concatenate.11, s32[1024]{0:T(1024)S(1)} %pad_clamp_fusion), kind=kCustom, calls=%fused_computation.3 | custom fusion | bytes 6032256 | tf_op jit(solution)/shard_map/jit(_take)/gather | solution.py:43
  120.4 4.6 %gather.18 = bf16[32,23,2048]{2,1,0:T(8,128)(2,1)} reshape(bf16[736,2048]{1,0:T(8,128)(2,1)} %gather_fusion.1) | data formatting | bytes 6029312 | tf_op jit(solution)/shard_map/jit(_take)/gather | solution.py:43
  125.0 3.9 broadcast_select_fusion
  129.0 36.2 %all-to-all-start.2 = ((bf16[32,23,2048]{2,1,0:T(8,128)(2,1)}), bf16[32,23,2048]{2,1,0:T(8,128)(2,1)}, u32[]{:S(2)}, u32[]{:S(2)}) async-start(bf16[32,23,2048]{2,1,0:T(8,128)(2,1)} %broadcast_select_fusion), calls=%async_computation.2 | async-start | bytes 6291456 | tf_op jit(solution)/shard_map/all_to_all | solution.py:114
  165.2 4.6 %reshape.244 = bf16[736,2048]{1,0:T(8,128)(2,1)} reshape(bf16[32,23,2048]{2,1,0:T(8,128)(2,1)} %all-to-all-done) | data formatting | bytes 6029312 | tf_op jit(solution)/shard_map/reshape | solution.py:47
  169.8 10.6 %fusion.2 = f32[736,1536]{1,0:T(8,128)} fusion(bf16[736,2048]{1,0:T(8,128)(2,1)} %reshape.244, bf16[1,1,2048,1536]{3,2,1,0:T(8,128)(2,1)} %param.14), kind=kOutput, calls=%fused_computation.7 | convolution fusion | flops 4630511616 | bytes 13828096 | tf_op jit(solution)/shard_map/dot_general | solution.py:48
  180.3 58.0 %all-to-all-done.2 = bf16[32,23,2048]{2,1,0:T(8,128)(2,1)} async-done(((bf16[32,23,2048]{2,1,0:T(8,128)(2,1)}), bf16[32,23,2048]{2,1,0:T(8,128)(2,1)}, u32[]{:S(2)}, u32[]{:S(2)}) %all-to-all-start.2) | async-done | bytes 3014688 | tf_op jit(solution)/shard_map/all_to_all | solution.py:114
  238.3 4.5 %reshape.248 = bf16[736,2048]{1,0:T(8,128)(2,1)} reshape(bf16[32,23,2048]{2,1,0:T(8,128)(2,1)} %all-to-all-done.2) | data formatting | bytes 6029312 | tf_op jit(solution)/shard_map/reshape | solution.py:57
  242.9 6.3 %multiply_convert_fusion.2 = (bf16[736,768]{1,0:T(8,128)(2,1)S(1)}, bf16[736,768]{1,0:T(8,128)(2,1)S(1)}) fusion(f32[736,1536]{1,0:T(8,128)} %fusion.2, bf16[736,2048]{1,0:T(8,128)(2,1)} %reshape.248, bf16[1,1,768,2048]{3,2,1,0:T(8,128)(2,1)S(1)} %copy-done), kind=kOutput, calls=%fused_computation.22 | convolution fusion | flops 2322604032 | bytes 12943360 | tf_op jit(solution)/shard_map/dot_general | solution.py:59
  249.2 9.0 %fusion.4 = bf16[736,2048]{1,0:T(8,128)(2,1)} fusion(bf16[1,1,2048,1536]{3,2,1,0:T(8,128)(2,1)} %param.14, bf16[736,768]{1,0:T(8,128)(2,1)S(1)} %get-tuple-element.20, bf16[736,768]{1,0:T(8,128)(2,1)S(1)} %get-tuple-element.19), kind=kOutput, calls=%fused_computation.12 | convolution fusion | flops 4636540928 | bytes 11567104 | tf_op jit(solution)/shard_map/dot_general | solution.py:72
  258.2 4.6 %reshape.249 = bf16[32,23,2048]{2,1,0:T(8,128)(2,1)} reshape(bf16[736,2048]{1,0:T(8,128)(2,1)} %fusion.4) | data formatting | bytes 6029312 | tf_op jit(solution)/shard_map/reshape | solution.py:75
  262.8 8.1 %all-to-all-start.3 = ((bf16[32,23,2048]{2,1,0:T(8,128)(2,1)}), bf16[32,23,2048]{2,1,0:T(8,128)(2,1)}, u32[]{:S(2)}, u32[]{:S(2)}) async-start(bf16[32,23,2048]{2,1,0:T(8,128)(2,1)} %reshape.249), calls=%async_computation.3 | async-start | bytes 6291456 | tf_op jit(solution)/shard_map/all_to_all | solution.py:116
  270.9 6.4 %convolution_convert_fusion = bf16[736,2048]{1,0:T(8,128)(2,1)} fusion(bf16[1,1,768,2048]{3,2,1,0:T(8,128)(2,1)S(1)} %copy-done, f32[736,1536]{1,0:T(8,128)} %fusion.2), kind=kOutput, calls=%fused_computation.11 | convolution fusion | flops 2320154624 | bytes 10682368 | tf_op jit(solution)/shard_map/dot_general | solution.py:52
  277.3 4.6 %reshape.245 = bf16[32,23,2048]{2,1,0:T(8,128)(2,1)} reshape(bf16[736,2048]{1,0:T(8,128)(2,1)} %convolution_convert_fusion) | data formatting | bytes 6029312 | tf_op jit(solution)/shard_map/reshape | solution.py:53
  281.9 49.3 %all-to-all-done.3 = bf16[32,23,2048]{2,1,0:T(8,128)(2,1)} async-done(((bf16[32,23,2048]{2,1,0:T(8,128)(2,1)}), bf16[32,23,2048]{2,1,0:T(8,128)(2,1)}, u32[]{:S(2)}, u32[]{:S(2)}) %all-to-all-start.3) | async-done | bytes 3014688 | tf_op jit(solution)/shard_map/all_to_all | solution.py:116
  331.1 19.1 %all-to-all-start.1 = ((bf16[32,23,2048]{2,1,0:T(8,128)(2,1)}), bf16[32,23,2048]{2,1,0:T(8,128)(2,1)}, u32[]{:S(2)}, u32[]{:S(2)}) async-start(bf16[32,23,2048]{2,1,0:T(8,128)(2,1)} %reshape.245), calls=%async_computation.1 | async-start | bytes 6291456 | tf_op jit(solution)/shard_map/all_to_all | solution.py:113
  350.3 4.5 %reshape.250 = bf16[736,2048]{1,0:T(8,128)(2,1)} reshape(bf16[32,23,2048]{2,1,0:T(8,128)(2,1)} %all-to-all-done.3) | data formatting | bytes 6029312 | tf_op jit(solution)/shard_map/reshape | solution.py:121
  354.8 7.5 %gather_fusion.3 = bf16[512,2048]{1,0:T(8,128)(2,1)} fusion(bf16[736,2048]{1,0:T(8,128)(2,1)} %reshape.250, s32[1024]{0:T(1024)S(1)} %pad_clamp_fusion.1), kind=kCustom, calls=%fused_computation.1.clone | custom fusion | bytes 4196352 | tf_op jit(solution)/shard_map/jit(_take)/gather | solution.py:121
  362.4 16.3 %all-to-all-done.1 = bf16[32,23,2048]{2,1,0:T(8,128)(2,1)} async-done(((bf16[32,23,2048]{2,1,0:T(8,128)(2,1)}), bf16[32,23,2048]{2,1,0:T(8,128)(2,1)}, u32[]{:S(2)}, u32[]{:S(2)}) %all-to-all-start.1) | async-done | bytes 3014688 | tf_op jit(solution)/shard_map/all_to_all | solution.py:113
  378.7 4.5 %reshape.246 = bf16[736,2048]{1,0:T(8,128)(2,1)} reshape(bf16[32,23,2048]{2,1,0:T(8,128)(2,1)} %all-to-all-done.1) | data formatting | bytes 6029312 | tf_op jit(solution)/shard_map/reshape | solution.py:118
  383.2 7.5 %gather_fusion.2 = bf16[512,2048]{1,0:T(8,128)(2,1)} fusion(bf16[736,2048]{1,0:T(8,128)(2,1)} %reshape.246, s32[1024]{0:T(1024)S(1)} %pad_clamp_fusion.1), kind=kCustom, calls=%fused_computation.clone | custom fusion | bytes 4196352 | tf_op jit(solution)/shard_map/jit(_take)/gather | solution.py:118
  390.7 4.6 %broadcast_select_fusion.2 = (bf16[512,2048]{1,0:T(8,128)(2,1)}, bf16[512,2048]{1,0:T(8,128)(2,1)}) fusion(bf16[512,2048]{1,0:T(8,128)(2,1)} %gather_fusion.3, pred[512]{0:T(512)(128)(4,1)S(1)} %get-tuple-element.13, bf16[512,2048]{1,0:T(8,128)(2,1)} %gather_fusion.2), kind=kLoop, calls=%fused_computation.25 | loop fusion | flops 2097152 | bytes 8389120 | tf_op jit(solution)/shard_map/jit(_take)/select_n | solution.py:121
  395.3 4.1 reshape.247
  399.4 4.5 %fusion.14 = f32[128,1,4]{2,1,0:T(1,128)S(1)} fusion(bf16[128,4,2048]{2,1,0:T(4,128)(2,1)} %reshape.247, bf16[128,2048,1]{1,0,2:T(8,128)(2,1)} %get-tuple-element.22), kind=kOutput, calls=%fused_computation.28 | convolution fusion | flops 2097152 | bytes 2623488 | tf_op jit(solution)/shard_map/tkd,td->tk/dot_general | solution.py:127
  404.8 5.7 %multiply_reduce_fusion = bf16[128,2048]{1,0:T(8,128)(2,1)} fusion(bf16[128,4,2048]{2,1,0:T(4,128)(2,1)} %reshape.247, f32[128,4]{1,0:T(8,128)S(1)} %copy.18), kind=kLoop, calls=%fused_computation.10 | loop fusion | flops 2883584 | bytes 2623488 | tf_op jit(solution)/shard_map/reduce_sum | solution.py:124
  410.5 4.1 reshape.251
  414.6 5.0 %reduce_sum.142 = bf16[128,2048]{1,0:T(8,128)(2,1)} reduce(bf16[128,4,2048]{2,1,0:T(4,128)(2,1)} %reshape.251, bf16[]{:T(256)} %constant.104.clone.1), dimensions={1}, to_apply=%region_15.17 | reduce | flops 786432 | bytes 2621442 | tf_op jit(solution)/shard_map/reduce_sum | solution.py:129
  (60 shorter events, 29.9 us)
Async XLA Ops:
  0.6 242.3 %copy-start = (bf16[1,1,768,2048]{3,2,1,0:T(8,128)(2,1)S(1)}, bf16[1,1,768,2048]{3,2,1,0:T(8,128)(2,1)}, u32[]{:S(2)}) copy-start(bf16[1,1,768,2048]{3,2,1,0:T(8,128)(2,1)} %param.15) | copy-start | bytes 9437188
  0.6 11.1 %collective-permute-start = (bf16[128,2048]{1,0:T(8,128)(2,1)}, bf16[128,2048]{1,0:T(8,128)(2,1)}, u32[]{:S(2)}, u32[]{:S(2)}) collective-permute-start(bf16[128,2048]{1,0:T(8,128)(2,1)} %bitcast.86), channel_id=1, source_target_pairs={{0,32},{32,64},{64,96},{96,128},{128,160},{160,192},{192,224},{1,3... | collective-permute-start | bytes 1572872 | tf_op jit(solution)/shard_map/ppermute | solution.py:10
  30.5 13.8 %copy-start.1 = (f32[1,128,4]{1,2,0:T(4,128)S(1)}, f32[1,128,4]{1,2,0:T(4,128)}, u32[]{:S(2)}) copy-start(f32[1,128,4]{1,2,0:T(4,128)} %param.12) | copy-start | bytes 6148
  30.5 98.5 %all-to-all-start = ((bf16[32,23,2048]{2,1,0:T(8,128)(2,1)}), bf16[32,23,2048]{2,1,0:T(8,128)(2,1)}, u32[]{:S(2)}, u32[]{:S(2)}) async-start(bf16[32,23,2048]{2,1,0:T(8,128)(2,1)} %broadcast_select_fusion.1), calls=%async_computation | async-start | bytes 6291456 | tf_op jit(solution)/shard_map/all_to_all | solution.py:108
  42.0 54.9 %collective-permute-start.1 = (bf16[128,2048]{1,0:T(8,128)(2,1)}, bf16[128,2048]{1,0:T(8,128)(2,1)}, u32[]{:S(2)}, u32[]{:S(2)}) collective-permute-start(bf16[128,2048]{1,0:T(8,128)(2,1)} %bitcast.87), channel_id=1, source_target_pairs={{32,0},{64,32},{96,64},{128,96},{160,128},{192,160},{224,192},{33,... | collective-permute-start | bytes 1572872 | tf_op jit(solution)/shard_map/ppermute | solution.py:10
  129.0 109.4 %all-to-all-start.2 = ((bf16[32,23,2048]{2,1,0:T(8,128)(2,1)}), bf16[32,23,2048]{2,1,0:T(8,128)(2,1)}, u32[]{:S(2)}, u32[]{:S(2)}) async-start(bf16[32,23,2048]{2,1,0:T(8,128)(2,1)} %broadcast_select_fusion), calls=%async_computation.2 | async-start | bytes 6291456 | tf_op jit(solution)/shard_map/all_to_all | solution.py:114
  262.8 68.4 %all-to-all-start.3 = ((bf16[32,23,2048]{2,1,0:T(8,128)(2,1)}), bf16[32,23,2048]{2,1,0:T(8,128)(2,1)}, u32[]{:S(2)}, u32[]{:S(2)}) async-start(bf16[32,23,2048]{2,1,0:T(8,128)(2,1)} %reshape.249), calls=%async_computation.3 | async-start | bytes 6291456 | tf_op jit(solution)/shard_map/all_to_all | solution.py:116
  331.1 47.6 %all-to-all-start.1 = ((bf16[32,23,2048]{2,1,0:T(8,128)(2,1)}), bf16[32,23,2048]{2,1,0:T(8,128)(2,1)}, u32[]{:S(2)}, u32[]{:S(2)}) async-start(bf16[32,23,2048]{2,1,0:T(8,128)(2,1)} %reshape.245), calls=%async_computation.1 | async-start | bytes 6291456 | tf_op jit(solution)/shard_map/all_to_all | solution.py:113
where the time goes:
time: 421 us; the launch traced here: 420 us
  waiting for transfers between devices  177 us (42%)
  local copies, waits for them, and re-layouts  92.5 us (22%)
  starting transfers between devices  79.4 us (19%)
  matrix products  36.8 us (9%)
  other arithmetic  33.2 us (8%)
    all_to_all x1, waiting for transfers between devices, local(): lax.all_to_all(grad_rows, 'expert', split_axis=0, concat_axis=0, tiled=True)  58 us
    ppermute x2, waiting for transfers between devices, passed_along(): return lax.ppermute(x, axis, pairs)  53.2 us
    all_to_all x1, waiting for transfers between devices, local(): lax.all_to_all(row_grad, 'expert', split_axis=0, concat_axis=0, tiled=True)  49.3 us
    all_to_all x1, starting transfers between devices, local(): lax.all_to_all(grad_rows, 'expert', split_axis=0, concat_axis=0, tiled=True)  36.2 us
    gather x4, local copies, waits for them, and re-layouts, pick_rows(): return jnp.take(padded, index, axis=0)  26.3 us
    all_to_all x1, starting transfers between devices, local(): lax.all_to_all(produced, 'expert', split_axis=0, concat_axis=0, tiled=True)  19.1 us
    all_to_all x1, waiting for transfers between devices, local(): lax.all_to_all(produced, 'expert', split_axis=0, concat_axis=0, tiled=True)  16.3 us
    all_to_all x1, starting transfers between devices, local(): lax.all_to_all(outgoing, 'expert', split_axis=0, concat_axis=0, tiled=True)  11.5 us
  transfers between devices with their start and end apart: 6, of which 5 were waited for; matrix products, arithmetic and copies ran while one was open for 19% of the time, Pallas kernels for 0%

commit v1 on v0

v1 whole, which is shorter than its diff:
```python
import functools

import jax
import jax.numpy as jnp
from jax import lax
from jax.experimental import pallas as pl
from jax.experimental.pallas import tpu as pltpu
from jax.sharding import Mesh, PartitionSpec as P

F32 = jnp.float32
BF16 = jnp.bfloat16
SECTION = ("z_lo", "core")
EXPERT = ("y", "z_hi", "x")
PLANE = ("y", "x")
SIZES = (4, 2, 4, 2, 4)
CAP = 24
VMEM_BYTES = 48 * 1024 * 1024
ANYWHERE = pl.BlockSpec(memory_space=pltpu.VMEM)
SCALAR = pl.BlockSpec(memory_space=pltpu.SMEM)


def dot(a, b, ca, cb):
    return lax.dot_general(a, b, (((ca,), (cb,)), ((), ())), preferred_element_type=F32)


def probabilities(meta):
    raised = jnp.exp(meta[4:8, :])
    return raised / jnp.sum(raised, axis=0, keepdims=True)


def row_marks(meta, table, half, rows):
    copies = table.shape[1]
    tokens = meta.shape[1]
    experts = copies - copies // 8
    ids = meta[0:4, :].astype(jnp.int32)
    label = lax.broadcasted_iota(jnp.int32, (copies, tokens), 0)
    named = [ids[k : k + 1, :] == label for k in range(4)]
    onehot = sum(n.astype(F32) for n in named).astype(BF16)
    earlier = (
        lax.broadcasted_iota(jnp.int32, (tokens, tokens), 0)
        < lax.broadcasted_iota(jnp.int32, (tokens, tokens), 1)
    ).astype(F32).astype(BF16)
    rank = dot(onehot, earlier, 1, 0).astype(jnp.int32)
    copy = lax.broadcasted_iota(jnp.int32, (copies, copies), 1)
    held = table == lax.broadcasted_iota(jnp.int32, (copies, copies), 0)
    first = jnp.sum(jnp.where(held & (copy < experts), copy, 0), axis=1, keepdims=True)
    second = jnp.sum(jnp.where(held & (copy >= experts), copy, 0), axis=1, keepdims=True)
    hot = second > 0
    target = jnp.where(hot & ((rank & 1) == 1), second, first)
    place = jnp.where(hot, rank >> 1, rank)
    row = ((target >> 3) * 4 + (target & 3)) * CAP + place
    row = jnp.where(((target >> 2) & 1) == half, row, -1)
    number = lax.broadcasted_iota(jnp.int32, (rows, tokens), 0)
    return [
        number == jnp.sum(jnp.where(n, row, 0), axis=0, keepdims=True) for n in named
    ]


def either(marks):
    return sum(m.astype(F32) for m in marks)


def weighted(marks, probs):
    return sum(jnp.where(m, probs[k : k + 1, :], 0.0) for k, m in enumerate(marks))


def pack_kernel(half_ref, meta_ref, table_ref, x_ref, out_ref, *, scaled):
    meta = meta_ref[...]
    marks = row_marks(meta, table_ref[...], half_ref[0], out_ref.shape[0])
    picked = dot(either(marks).astype(BF16), x_ref[...], 1, 0)
    if scaled:
        weight = jnp.sum(weighted(marks, probabilities(meta)), axis=1, keepdims=True)
        picked = picked * weight
    out_ref[...] = picked.astype(BF16)


def pack(half, meta, table, x, scaled):
    rows = 16 * CAP
    return pl.pallas_call(
        functools.partial(pack_kernel, scaled=scaled),
        out_shape=jax.ShapeDtypeStruct((rows, x.shape[1]), BF16),
        in_specs=[SCALAR, ANYWHERE, ANYWHERE, ANYWHERE],
        out_specs=ANYWHERE,
        compiler_params=pltpu.CompilerParams(vmem_limit_bytes=VMEM_BYTES),
        cost_estimate=pl.CostEstimate(
            flops=2 * rows * x.size, bytes_accessed=2 * x.size + 2 * rows * x.shape[1], transcendentals=0
        ),
        name="pack_grad" if scaled else "pack_in",
    )(half, meta, table, x)


def split_dot(weights, rows):
    high = weights.astype(BF16)
    low = (weights - high.astype(F32)).astype(BF16)
    return dot(high, rows, 0, 0) + dot(low, rows, 0, 0)


def out_kernel(half_ref, meta_ref, table_ref, rows_ref, g_ref, *refs, last):
    meta = meta_ref[...]
    rows = rows_ref[...]
    marks = row_marks(meta, table_ref[...], half_ref[0], rows.shape[0])
    probs = probabilities(meta)
    total = split_dot(weighted(marks, probs), rows)
    products = dot(rows, g_ref[...], 1, 1)
    grads = jnp.concatenate(
        [jnp.sum(jnp.where(m, products, 0.0), axis=0, keepdims=True) for m in marks], axis=0
    )
    if last:
        other_ref, other_grads_ref, out_ref, logit_ref = refs
        out_ref[...] = (total + other_ref[...].astype(F32)).astype(BF16)
        grads = grads + other_grads_ref[0:4, :]
        logit_ref[...] = probs * (grads - jnp.sum(probs * grads, axis=0, keepdims=True))
    else:
        out_ref, grads_ref = refs
        out_ref[...] = total.astype(BF16)
        grads_ref[...] = jnp.concatenate([grads, jnp.zeros_like(grads)], axis=0)


def collect_out(half, meta, table, rows, g, other=None):
    last = other is not None
    extra = list(other) if last else []
    return pl.pallas_call(
        functools.partial(out_kernel, last=last),
        out_shape=(
            jax.ShapeDtypeStruct(g.shape, BF16),
            jax.ShapeDtypeStruct((4 if last else 8, g.shape[0]), F32),
        ),
        in_specs=[SCALAR] + [ANYWHERE] * (4 + len(extra)),
        out_specs=(ANYWHERE, ANYWHERE),
        compiler_params=pltpu.CompilerParams(vmem_limit_bytes=VMEM_BYTES),
        cost_estimate=pl.CostEstimate(
            flops=6 * rows.shape[0] * g.size, bytes_accessed=2 * rows.size + 4 * g.size, transcendentals=0
        ),
        name="collect_out_last" if last else "collect_out",
    )(half, meta, table, rows, g, *extra)


def grad_kernel(half_ref, meta_ref, table_ref, rows_ref, *refs, last):
    rows = rows_ref[...]
    marks = row_marks(meta_ref[...], table_ref[...], half_ref[0], rows.shape[0])
    total = dot(either(marks).astype(BF16), rows, 0, 0)
    if last:
        total = total + refs[0][...].astype(F32)
    refs[-1][...] = total.astype(BF16)


def collect_grad(half, meta, table, rows, other=None):
    last = other is not None
    extra = [other] if last else []
    tokens = meta.shape[1]
    return pl.pallas_call(
        functools.partial(grad_kernel, last=last),
        out_shape=jax.ShapeDtypeStruct((tokens, rows.shape[1]), BF16),
        in_specs=[SCALAR] + [ANYWHERE] * (3 + len(extra)),
        out_specs=ANYWHERE,
        compiler_params=pltpu.CompilerParams(vmem_limit_bytes=VMEM_BYTES),
        cost_estimate=pl.CostEstimate(
            flops=2 * rows.size * tokens, bytes_accessed=2 * rows.size + 2 * tokens * rows.shape[1], transcendentals=0
        ),
        name="collect_grad_last" if last else "collect_grad",
    )(half, meta, table, rows, *extra)


def forward_kernel(x_ref, wg_ref, wu_ref, wd_ref, out_ref, gate_ref, up_ref, total):
    step = pl.program_id(0)
    x = x_ref[...]
    gate = dot(x, wg_ref[...], 1, 0)
    up = dot(x, wu_ref[...], 1, 0)
    gate_ref[...] = gate
    up_ref[...] = up
    hidden = (gate * jax.nn.sigmoid(gate) * up).astype(BF16)
    part = dot(hidden, wd_ref[...], 1, 0)

    @pl.when(step == 0)
    def _():
        total[...] = part

    @pl.when(step > 0)
    def _():
        total[...] += part

    @pl.when(step == pl.num_programs(0) - 1)
    def _():
        out_ref[...] = total[...].astype(BF16)


def backward_kernel(g_ref, gate_ref, up_ref, wg_ref, wu_ref, wd_ref, out_ref, total):
    step = pl.program_id(0)
    hidden_grad = dot(g_ref[...], wd_ref[...], 1, 1)
    gate = gate_ref[...]
    up = up_ref[...]
    sigmoid = jax.nn.sigmoid(gate)
    gate_grad = (hidden_grad * up * sigmoid * (1.0 + gate * (1.0 - sigmoid))).astype(BF16)
    up_grad = (hidden_grad * gate * sigmoid).astype(BF16)
    part = dot(gate_grad, wg_ref[...], 1, 1) + dot(up_grad, wu_ref[...], 1, 1)

    @pl.when(step == 0)
    def _():
        total[...] = part

    @pl.when(step > 0)
    def _():
        total[...] += part

    @pl.when(step == pl.num_programs(0) - 1)
    def _():
        out_ref[...] = total[...].astype(BF16)


BLOCK = 256


def expert_specs(rows, width, hidden):
    steps = hidden // BLOCK
    whole = pl.BlockSpec((rows, width), lambda j: (0, 0))
    gate = pl.BlockSpec((width, BLOCK), lambda j: (0, j))
    up = pl.BlockSpec((width, BLOCK), lambda j: (0, steps + j))
    down = pl.BlockSpec((BLOCK, width), lambda j: (j, 0))
    pre = pl.BlockSpec((rows, BLOCK), lambda j: (0, j))
    return steps, whole, gate, up, down, pre


def expert_cost(rows, width, hidden):
    return pl.CostEstimate(
        flops=6 * rows * width * hidden,
        bytes_accessed=6 * width * hidden + 4 * rows * width + 8 * rows * hidden,
        transcendentals=rows * hidden,
    )


def expert_forward(x, w_gu, w_dn):
    rows, width = x.shape
    hidden = w_dn.shape[0]
    steps, whole, gate, up, down, pre = expert_specs(rows, width, hidden)
    return pl.pallas_call(
        forward_kernel,
        grid=(steps,),
        out_shape=(
            jax.ShapeDtypeStruct((rows, width), BF16),
            jax.ShapeDtypeStruct((rows, hidden), F32),
            jax.ShapeDtypeStruct((rows, hidden), F32),
        ),
        in_specs=[whole, gate, up, down],
        out_specs=(whole, pre, pre),
        scratch_shapes=[pltpu.VMEM((rows, width), F32)],
        compiler_params=pltpu.CompilerParams(vmem_limit_bytes=VMEM_BYTES),
        cost_estimate=expert_cost(rows, width, hidden),
        name="expert_forward",
    )(x, w_gu, w_gu, w_dn)


def expert_backward(g, gates, ups, w_gu, w_dn):
    rows, width = g.shape
    hidden = w_dn.shape[0]
    steps, whole, gate, up, down, pre = expert_specs(rows, width, hidden)
    return pl.pallas_call(
        backward_kernel,
        grid=(steps,),
        out_shape=jax.ShapeDtypeStruct((rows, width), BF16),
        in_specs=[whole, pre, pre, gate, up, down],
        out_specs=whole,
        scratch_shapes=[pltpu.VMEM((rows, width), F32)],
        compiler_params=pltpu.CompilerParams(vmem_limit_bytes=VMEM_BYTES),
        cost_estimate=expert_cost(rows, width, hidden),
        name="expert_backward",
    )(g, gates, ups, w_gu, w_gu, w_dn)


def passed_along(x, by):
    devices = SIZES[0] * SIZES[1]
    pairs = [(i, i + by) for i in range(devices) if 0 <= i + by < devices]
    return lax.ppermute(x, SECTION, pairs)


def swapped(x):
    return lax.ppermute(x, "z_hi", [(0, 1), (1, 0)])


def exchanged(rows):
    width = rows.shape[-1]
    moved = lax.all_to_all(
        rows.reshape(16, CAP, width), PLANE, split_axis=0, concat_axis=0, tiled=True
    )
    return moved.reshape(16 * CAP, width)


def local(x_held, grad_held, expert_ids, gate_logits, placement, w_gate_up, w_down):
    own_x = x_held[0]
    own_g = grad_held[0]
    w_gu = w_gate_up[0, 0]
    w_dn = w_down[0, 0]
    section = lax.axis_index(SECTION)
    sections = SIZES[0] * SIZES[1]
    half = lax.axis_index("z_hi").astype(jnp.int32).reshape(1)
    table = placement

    meta = jnp.concatenate([expert_ids[0].astype(F32).T, gate_logits[0].T], axis=0)
    meta_other = swapped(meta)
    x = jnp.where(section == 0, own_x, passed_along(own_x, 1))
    g = jnp.where(section == sections - 1, own_g, passed_along(own_g, -1))
    x_other = swapped(x)
    g_other = swapped(g)

    x_rows = exchanged(pack(half, meta, table, x, False))
    x_rows_other = exchanged(pack(half, meta_other, table, x_other, False))
    g_rows = exchanged(pack(half, meta, table, g, True))
    g_rows_other = exchanged(pack(half, meta_other, table, g_other, True))

    out, gate, up = expert_forward(x_rows, w_gu, w_dn)
    out_other, gate_other, up_other = expert_forward(x_rows_other, w_gu, w_dn)
    out_other = exchanged(out_other)
    out = exchanged(out)
    back_other = exchanged(expert_backward(g_rows_other, gate_other, up_other, w_gu, w_dn))
    back = exchanged(expert_backward(g_rows, gate, up, w_gu, w_dn))

    part, part_grads = collect_out(half, meta_other, table, out_other, g_other)
    part = swapped(part)
    part_grads = swapped(part_grads)
    back_part = swapped(collect_grad(half, meta_other, table, back_other))
    section_out, logit_grad = collect_out(half, meta, table, out, g, (part, part_grads))
    input_grad = collect_grad(half, meta, table, back, back_part)
    return section_out[None], input_grad[None], logit_grad.T[None]


def solution(mesh):
    fine = Mesh(mesh.devices.reshape(SIZES), SECTION + EXPERT)
    placed = (
        P(SECTION, EXPERT, None),
        P(SECTION, EXPERT, None),
        P(SECTION, EXPERT, None),
        P(SECTION, EXPERT, None),
        P(SECTION, None),
        P(SECTION, EXPERT, None, None),
        P(SECTION, EXPERT, None, None),
    )
    return jax.shard_map(
        local,
        mesh=fine,
        in_specs=placed,
        out_specs=(P(SECTION, EXPERT, None),) * 3,
        check_vma=False,
    )
```

time: 421 us -> 264 us (0.63)
  the two profiles are of different devices: /device:TPU:96 before, /device:TPU:66 now
where the time goes in v1:
time: 264 us; the launch traced here: 262 us
  waiting for transfers between devices  94.2 us (36%)
  starting transfers between devices  72.8 us (28%)
  Pallas kernels  49.2 us (19%)
  blocking collectives  26.4 us (10%)
  local copies, waits for them, and re-layouts  16.6 us (6%)
    ppermute x6, waiting for transfers between devices, swapped(): return lax.ppermute(x, 'z_hi', [(0, 1), (1, 0)])  50.6 us
    all_to_all x7, starting transfers between devices, exchanged(): lax.all_to_all(rows.reshape(16, CAP, width), PLANE, split_axis=0, concat_...  46.5 us
    all_to_all x7, waiting for transfers between devices, exchanged(): lax.all_to_all(rows.reshape(16, CAP, width), PLANE, split_axis=0, concat_...  29.5 us
    all_to_all x1, blocking collectives, exchanged(): lax.all_to_all(rows.reshape(16, CAP, width), PLANE, split_axis=0, concat_...  26.4 us
    ppermute x6, starting transfers between devices, swapped(): return lax.ppermute(x, 'z_hi', [(0, 1), (1, 0)])  22.5 us
    pallas_call x2, Pallas kernels, expert_backward(): pl.pallas_call(backward_kernel, grid=(steps,), out_shape=jax.ShapeDtypeSt...  20.3 us
    unnamed x38, local copies, waits for them, and re-layouts  16.6 us
    pallas_call x2, Pallas kernels, expert_forward(): pl.pallas_call(forward_kernel, grid=(steps,), out_shape=(jax.ShapeDtypeSt...  15.1 us
  transfers between devices with their start and end apart: 15, of which 10 were waited for; matrix products, arithmetic and copies ran while one was open for 1% of the time, Pallas kernels for 17%

profile of v1, /device:TPU:66, one launch (start us, length us, event | category | flops | bytes accessed | tf_op | source)
XLA Modules:
  0.0 262.5 jit_solution(5368646066591581184)
XLA Ops:
  0.6 1.9 collective-permute-start
  4.0 7.4 %collective-permute-done = bf16[128,2048]{1,0:T(8,128)(2,1)S(1)} collective-permute-done((bf16[128,2048]{1,0:T(8,128)(2,1)}, bf16[128,2048]{1,0:T(8,128)(2,1)S(1)}, u32[]{:S(2)}, u32[]{:S(2)}) %collective-permute-start) | collective-permute-done | bytes 524320 | tf_op jit(solution)/shard_map/ppermute | solution.py:272
  12.5 1.9 pack_in.2
  15.2 7.6 %all-to-all-start = ((bf16[16,24,2048]{2,1,0:T(8,128)(2,1)}), bf16[16,24,2048]{2,1,0:T(8,128)(2,1)S(1)}, u32[]{:S(2)}, u32[]{:S(2)}) async-start(bf16[16,24,2048]{2,1,0:T(8,128)(2,1)} %bitcast.6), calls=%async_computation | async-start | bytes 3145728 | tf_op jit(solution)/shard_map/all_to_all | solution.py:281
  22.8 1.9 collective-permute-start.1
  24.7 6.7 %collective-permute-done.1 = bf16[128,2048]{1,0:T(8,128)(2,1)S(1)} collective-permute-done((bf16[128,2048]{1,0:T(8,128)(2,1)S(1)}, bf16[128,2048]{1,0:T(8,128)(2,1)S(1)}, u32[]{:S(2)}, u32[]{:S(2)}) %collective-permute-start.1) | collective-permute-done | bytes 524320 | tf_op jit(solution)/shard_map/ppermute | solution.py:272
  31.4 1.9 pack_grad.2
  34.1 10.0 %all-to-all-done = bf16[16,24,2048]{2,1,0:T(8,128)(2,1)S(1)} async-done(((bf16[16,24,2048]{2,1,0:T(8,128)(2,1)}), bf16[16,24,2048]{2,1,0:T(8,128)(2,1)S(1)}, u32[]{:S(2)}, u32[]{:S(2)}) %all-to-all-start) | async-done | bytes 1572896 | tf_op jit(solution)/shard_map/all_to_all | solution.py:281
  44.1 6.4 %all-to-all-start.4 = ((bf16[16,24,2048]{2,1,0:T(8,128)(2,1)}), bf16[16,24,2048]{2,1,0:T(8,128)(2,1)S(1)}, u32[]{:S(2)}, u32[]{:S(2)}) async-start(bf16[16,24,2048]{2,1,0:T(8,128)(2,1)} %bitcast.18), calls=%async_computation.4 | async-start | bytes 3145728 | tf_op jit(solution)/shard_map/all_to_all | solution.py:281
  50.5 3.6 %collective-permute-start.3 = (bf16[128,2048]{1,0:T(8,128)(2,1)}, bf16[128,2048]{1,0:T(8,128)(2,1)S(1)}, u32[]{:S(2)}, u32[]{:S(2)}) collective-permute-start(bf16[128,2048]{1,0:T(8,128)(2,1)} %copy-done.8), channel_id=1, source_target_pairs={{0,4},{4,0},{1,5},{5,1},{2,6},{6,2},{3,7},{7,3},{8,12},{12,8},{9,1... | collective-permute-start | bytes 1572872 | tf_op jit(solution)/shard_map/ppermute | solution.py:276
  54.2 2.3 collective-permute-start.2
  56.5 14.9 %collective-permute-done.2.meta_ref = f32[8,128]{1,0:T(8,128)S(1)} collective-permute-done((f32[8,128]{1,0:T(8,128)S(1)}, f32[8,128]{1,0:T(8,128)S(1)}, u32[]{:S(2)}, u32[]{:S(2)}) %collective-permute-start.2) | collective-permute-done | bytes 4128 | tf_op jit(solution)/shard_map/ppermute | solution.py:276
  74.5 7.2 %all-to-all-start.2 = ((bf16[16,24,2048]{2,1,0:T(8,128)(2,1)}), bf16[16,24,2048]{2,1,0:T(8,128)(2,1)S(1)}, u32[]{:S(2)}, u32[]{:S(2)}) async-start(bf16[16,24,2048]{2,1,0:T(8,128)(2,1)} %bitcast.39), calls=%async_computation.2 | async-start | bytes 3145728 | tf_op jit(solution)/shard_map/all_to_all | solution.py:281
  81.7 5.3 %collective-permute-start.4 = (bf16[128,2048]{1,0:T(8,128)(2,1)}, bf16[128,2048]{1,0:T(8,128)(2,1)S(1)}, u32[]{:S(2)}, u32[]{:S(2)}) collective-permute-start(bf16[128,2048]{1,0:T(8,128)(2,1)} %copy-done.6), channel_id=1, source_target_pairs={{0,4},{4,0},{1,5},{5,1},{2,6},{6,2},{3,7},{7,3},{8,12},{12,8},{9,1... | collective-permute-start | bytes 1572872 | tf_op jit(solution)/shard_map/ppermute | solution.py:276
  87.1 17.7 %collective-permute-done.4.g_ref.x_ref = bf16[128,2048]{1,0:T(8,128)(2,1)S(1)} collective-permute-done((bf16[128,2048]{1,0:T(8,128)(2,1)}, bf16[128,2048]{1,0:T(8,128)(2,1)S(1)}, u32[]{:S(2)}, u32[]{:S(2)}) %collective-permute-start.4) | collective-permute-done | bytes 524320 | tf_op jit(solution)/shard_map/ppermute | solution.py:276
  107.5 7.2 %all-to-all-start.6 = ((bf16[16,24,2048]{2,1,0:T(8,128)(2,1)}), bf16[16,24,2048]{2,1,0:T(8,128)(2,1)}, u32[]{:S(2)}, u32[]{:S(2)}) async-start(bf16[16,24,2048]{2,1,0:T(8,128)(2,1)} %bitcast.40), calls=%async_computation.6 | async-start | bytes 3145728 | tf_op jit(solution)/shard_map/all_to_all | solution.py:281
  114.7 7.6 %expert_forward.2 = (bf16[384,2048]{1,0:T(8,128)(2,1)S(1)}, f32[384,768]{1,0:T(8,128)S(1)}, f32[384,768]{1,0:T(8,128)S(1)}) custom-call(bf16[384,2048]{1,0:T(8,128)(2,1)S(1)} %bitcast.35, bf16[2048,1536]{1,0:T(8,128)(2,1)} %bitcast.47, bf16[2048,1536]{1,0:T(8,128)(2,1)} %bitcast.48, bf16[768,2048]{1,0:T(8,128)(2,1)} %bitcast.55), custom_call_target="tpu_custom_call" | custom-call | flops 3623878656 | bytes 14942208 | tf_op jit(solution)/shard_map/expert_forward/pallas_call | solution.py:235
  123.5 9.9 %expert_backward.2 = bf16[384,2048]{1,0:T(8,128)(2,1)S(1)} custom-call(bf16[384,2048]{1,0:T(8,128)(2,1)S(1)} %bitcast.42, f32[384,768]{1,0:T(8,128)S(1)} %get-tuple-element.18.gate_ref, f32[384,768]{1,0:T(8,128)S(1)} %get-tuple-element.19.up_ref, bf16[2048,1536]{1,0:T(8,128)(2,1)} %bitcast.49, bf16[2048,1536]{1,0:T(8,128)(2,1)} %bitcast.50, ...), custom_call_target="tpu_custom_call" | custom-call | flops 3623878656 | bytes 14942208 | tf_op jit(solution)/shard_map/expert_backward/pallas_call | solution.py:256
  136.2 6.5 %all-to-all-start.5 = ((bf16[16,24,2048]{2,1,0:T(8,128)(2,1)}), bf16[16,24,2048]{2,1,0:T(8,128)(2,1)S(1)}, u32[]{:S(2)}, u32[]{:S(2)}) async-start(bf16[16,24,2048]{2,1,0:T(8,128)(2,1)} %bitcast.43), calls=%async_computation.5 | async-start | bytes 3145728 | tf_op jit(solution)/shard_map/all_to_all | solution.py:281
  142.7 7.5 %expert_forward.3 = (bf16[384,2048]{1,0:T(8,128)(2,1)S(1)}, f32[384,768]{1,0:T(8,128)S(1)}, f32[384,768]{1,0:T(8,128)S(1)}) custom-call(bf16[384,2048]{1,0:T(8,128)(2,1)S(1)} %bitcast.38, bf16[2048,1536]{1,0:T(8,128)(2,1)} %bitcast.51, bf16[2048,1536]{1,0:T(8,128)(2,1)} %bitcast.52, bf16[768,2048]{1,0:T(8,128)(2,1)} %bitcast.57), custom_call_target="tpu_custom_call" | custom-call | flops 3623878656 | bytes 14942208 | tf_op jit(solution)/shard_map/expert_forward/pallas_call | solution.py:235
  153.5 10.1 %all-to-all-done.5 = bf16[16,24,2048]{2,1,0:T(8,128)(2,1)S(1)} async-done(((bf16[16,24,2048]{2,1,0:T(8,128)(2,1)}), bf16[16,24,2048]{2,1,0:T(8,128)(2,1)S(1)}, u32[]{:S(2)}, u32[]{:S(2)}) %all-to-all-start.5) | async-done | bytes 1572896 | tf_op jit(solution)/shard_map/all_to_all | solution.py:281
  163.6 6.5 %all-to-all-start.3 = ((bf16[16,24,2048]{2,1,0:T(8,128)(2,1)}), bf16[16,24,2048]{2,1,0:T(8,128)(2,1)}, u32[]{:S(2)}, u32[]{:S(2)}) async-start(bf16[16,24,2048]{2,1,0:T(8,128)(2,1)} %bitcast.46), calls=%async_computation.3 | async-start | bytes 3145728 | tf_op jit(solution)/shard_map/all_to_all | solution.py:281
  172.7 10.4 %expert_backward.3 = bf16[384,2048]{1,0:T(8,128)(2,1)S(1)} custom-call(bf16[384,2048]{1,0:T(8,128)(2,1)} %bitcast.23.g_ref, f32[384,768]{1,0:T(8,128)S(1)} %copy-done.12, f32[384,768]{1,0:T(8,128)S(1)} %copy-done.14, bf16[2048,1536]{1,0:T(8,128)(2,1)} %bitcast.53, bf16[2048,1536]{1,0:T(8,128)(2,1)} %bitcast.54, bf16[768,2048]{1,0:T(8,128)(2,1)} %bitcast.58), custom_call_target="tpu_custom_call" | custom-call | flops 3623878656 | bytes 14942208 | tf_op jit(solution)/shard_map/expert_backward/pallas_call | solution.py:256
  183.1 7.8 %all-to-all-done.3 = bf16[16,24,2048]{2,1,0:T(8,128)(2,1)} async-done(((bf16[16,24,2048]{2,1,0:T(8,128)(2,1)}), bf16[16,24,2048]{2,1,0:T(8,128)(2,1)}, u32[]{:S(2)}, u32[]{:S(2)}) %all-to-all-start.3) | async-done | bytes 1572896 | tf_op jit(solution)/shard_map/all_to_all | solution.py:281
  191.0 26.4 %all_to_all.40 = bf16[16,24,2048]{2,1,0:T(8,128)(2,1)} all-to-all(bf16[16,24,2048]{2,1,0:T(8,128)(2,1)S(1)} %bitcast.44), channel_id=1, replica_groups=mesh['z_lo'=4,'core'=2,'y'=4,'z_hi'=2,'x'=4] {'y','x'}, dimensions={0} | all-to-all | bytes 3145728 | tf_op jit(solution)/shard_map/all_to_all | solution.py:281
  217.3 5.0 %all-to-all-start.1 = ((bf16[16,24,2048]{2,1,0:T(8,128)(2,1)}), bf16[16,24,2048]{2,1,0:T(8,128)(2,1)S(1)}, u32[]{:S(2)}, u32[]{:S(2)}) async-start(bf16[16,24,2048]{2,1,0:T(8,128)(2,1)} %bitcast.45), calls=%async_computation.1 | async-start | bytes 3145728 | tf_op jit(solution)/shard_map/all_to_all | solution.py:281
  224.4 5.3 %collective-permute-start.7 = (bf16[128,2048]{1,0:T(8,128)(2,1)S(1)}, bf16[128,2048]{1,0:T(8,128)(2,1)S(1)}, u32[]{:S(2)}, u32[]{:S(2)}) collective-permute-start(bf16[128,2048]{1,0:T(8,128)(2,1)S(1)} %collect_grad.1), channel_id=1, source_target_pairs={{0,4},{4,0},{1,5},{5,1},{2,6},{6,2},{3,7},{7,3},{8,12},{12,8},{9,1... | collective-permute-start | bytes 1572872 | tf_op jit(solution)/shard_map/ppermute | solution.py:276
  229.7 3.3 %collect_out.1 = (bf16[128,2048]{1,0:T(8,128)(2,1)}, f32[8,128]{1,0:T(8,128)S(1)}) custom-call(s32[1]{0:T(128)} %bitcast.half_ref, f32[8,128]{1,0:T(8,128)S(1)} %collective-permute-done.2.meta_ref, s32[1,32]{1,0:T(1,128)S(1)} %copy-done.17, bf16[384,2048]{1,0:T(8,128)(2,1)} %bitcast.16.rows_ref, bf16[128,2048]{1,0:T(8,128)(2,1)S(1)} %copy-done.16), custom_call_target="tpu_custom_call" | custom-call | flops 603979776 | bytes 2621440 | tf_op jit(solution)/shard_map/collect_out/pallas_call | solution.py:122
  233.7 5.2 %collective-permute-start.6 = (f32[8,128]{1,0:T(8,128)S(1)}, f32[8,128]{1,0:T(8,128)S(1)}, u32[]{:S(2)}, u32[]{:S(2)}) collective-permute-start(f32[8,128]{1,0:T(8,128)S(1)} %get-tuple-element.16), channel_id=1, source_target_pairs={{0,4},{4,0},{1,5},{5,1},{2,6},{6,2},{3,7},{7,3},{8,12},{12,8},{9,1... | collective-permute-start | bytes 12296 | tf_op jit(solution)/shard_map/ppermute | solution.py:276
  238.9 9.3 %collective-permute-done.7.refs_0_ = bf16[128,2048]{1,0:T(8,128)(2,1)S(1)} collective-permute-done((bf16[128,2048]{1,0:T(8,128)(2,1)S(1)}, bf16[128,2048]{1,0:T(8,128)(2,1)S(1)}, u32[]{:S(2)}, u32[]{:S(2)}) %collective-permute-start.7) | collective-permute-done | bytes 524320 | tf_op jit(solution)/shard_map/ppermute | solution.py:276
  249.8 8.6 %collective-permute-done.6.refs_1_ = f32[8,128]{1,0:T(8,128)S(1)} collective-permute-done((f32[8,128]{1,0:T(8,128)S(1)}, f32[8,128]{1,0:T(8,128)S(1)}, u32[]{:S(2)}, u32[]{:S(2)}) %collective-permute-start.6) | collective-permute-done | bytes 4128 | tf_op jit(solution)/shard_map/ppermute | solution.py:276
  259.4 3.1 %collect_out_last.1 = (bf16[128,2048]{1,0:T(8,128)(2,1)}, f32[4,128]{1,0:T(4,128)}) custom-call(s32[1]{0:T(128)} %bitcast.half_ref, f32[8,128]{1,0:T(8,128)S(1)} %pad_maximum_fusion.meta_ref, s32[1,32]{1,0:T(1,128)S(1)} %copy-done.17, bf16[384,2048]{1,0:T(8,128)(2,1)S(1)} %bitcast.37, bf16[128,2048]{1,0:T(8,128)(2,1)S(1)} %copy-done.7, ...), custom_call_target="tpu_custom_call" | custom-call | flops 603979776 | bytes 2621440 | tf_op jit(solution)/shard_map/collect_out_last/pallas_call | solution.py:122
  (53 shorter events, 25.1 us)
Async XLA Ops:
  0.6 11.8 %copy-start.17 = (s32[1,32]{1,0:T(1,128)S(1)}, s32[1,32]{1,0:T(1,128)}, u32[]{:S(2)}) copy-start(s32[1,32]{1,0:T(1,128)} %table_ref.15) | copy-start | bytes 388
  0.6 10.7 %collective-permute-start = (bf16[128,2048]{1,0:T(8,128)(2,1)}, bf16[128,2048]{1,0:T(8,128)(2,1)S(1)}, u32[]{:S(2)}, u32[]{:S(2)}) collective-permute-start(bf16[128,2048]{1,0:T(8,128)(2,1)} %bitcast.60), channel_id=1, source_target_pairs={{0,32},{32,64},{64,96},{96,128},{128,160},{160,192},{192,224},{1,3... | collective-permute-start | bytes 1572872 | tf_op jit(solution)/shard_map/ppermute | solution.py:272
  14.4 0.8 copy-start.8
  15.2 7.6 %copy-start.18 = (bf16[1,128,2048]{2,1,0:T(8,128)(2,1)S(1)}, bf16[1,128,2048]{2,1,0:T(8,128)(2,1)}, u32[]{:S(2)}) copy-start(bf16[1,128,2048]{2,1,0:T(8,128)(2,1)} %param.8) | copy-start | bytes 1572868
  15.2 28.9 %all-to-all-start = ((bf16[16,24,2048]{2,1,0:T(8,128)(2,1)}), bf16[16,24,2048]{2,1,0:T(8,128)(2,1)S(1)}, u32[]{:S(2)}, u32[]{:S(2)}) async-start(bf16[16,24,2048]{2,1,0:T(8,128)(2,1)} %bitcast.6), calls=%async_computation | async-start | bytes 3145728 | tf_op jit(solution)/shard_map/all_to_all | solution.py:281
  22.8 8.6 %collective-permute-start.1 = (bf16[128,2048]{1,0:T(8,128)(2,1)S(1)}, bf16[128,2048]{1,0:T(8,128)(2,1)S(1)}, u32[]{:S(2)}, u32[]{:S(2)}) collective-permute-start(bf16[128,2048]{1,0:T(8,128)(2,1)S(1)} %bitcast.61), channel_id=1, source_target_pairs={{32,0},{64,32},{96,64},{128,96},{160,128},{192,160},{224,192},{33,... | collective-permute-start | bytes 1572872 | tf_op jit(solution)/shard_map/ppermute | solution.py:272
  44.1 29.2 %all-to-all-start.4 = ((bf16[16,24,2048]{2,1,0:T(8,128)(2,1)}), bf16[16,24,2048]{2,1,0:T(8,128)(2,1)S(1)}, u32[]{:S(2)}, u32[]{:S(2)}) async-start(bf16[16,24,2048]{2,1,0:T(8,128)(2,1)} %bitcast.18), calls=%async_computation.4 | async-start | bytes 3145728 | tf_op jit(solution)/shard_map/all_to_all | solution.py:281
  50.5 20.9 %collective-permute-start.3 = (bf16[128,2048]{1,0:T(8,128)(2,1)}, bf16[128,2048]{1,0:T(8,128)(2,1)S(1)}, u32[]{:S(2)}, u32[]{:S(2)}) collective-permute-start(bf16[128,2048]{1,0:T(8,128)(2,1)} %copy-done.8), channel_id=1, source_target_pairs={{0,4},{4,0},{1,5},{5,1},{2,6},{6,2},{3,7},{7,3},{8,12},{12,8},{9,1... | collective-permute-start | bytes 1572872 | tf_op jit(solution)/shard_map/ppermute | solution.py:276
  54.2 17.2 %collective-permute-start.2 = (f32[8,128]{1,0:T(8,128)S(1)}, f32[8,128]{1,0:T(8,128)S(1)}, u32[]{:S(2)}, u32[]{:S(2)}) collective-permute-start(f32[8,128]{1,0:T(8,128)S(1)} %pad_maximum_fusion.meta_ref), channel_id=1, source_target_pairs={{0,4},{4,0},{1,5},{5,1},{2,6},{6,2},{3,7},{7,3},{8,12},{12,8},{9,1... | collective-permute-start | bytes 12296 | tf_op jit(solution)/shard_map/ppermute | solution.py:276
  72.1 1.2 copy-start
  73.3 1.2 copy-start.3
  74.5 33.0 %all-to-all-start.2 = ((bf16[16,24,2048]{2,1,0:T(8,128)(2,1)}), bf16[16,24,2048]{2,1,0:T(8,128)(2,1)S(1)}, u32[]{:S(2)}, u32[]{:S(2)}) async-start(bf16[16,24,2048]{2,1,0:T(8,128)(2,1)} %bitcast.39), calls=%async_computation.2 | async-start | bytes 3145728 | tf_op jit(solution)/shard_map/all_to_all | solution.py:281
  81.7 23.0 %collective-permute-start.4 = (bf16[128,2048]{1,0:T(8,128)(2,1)}, bf16[128,2048]{1,0:T(8,128)(2,1)S(1)}, u32[]{:S(2)}, u32[]{:S(2)}) collective-permute-start(bf16[128,2048]{1,0:T(8,128)(2,1)} %copy-done.6), channel_id=1, source_target_pairs={{0,4},{4,0},{1,5},{5,1},{2,6},{6,2},{3,7},{7,3},{8,12},{12,8},{9,1... | collective-permute-start | bytes 1572872 | tf_op jit(solution)/shard_map/ppermute | solution.py:276
  105.5 1.2 copy-start.1
  107.5 28.7 %all-to-all-start.6 = ((bf16[16,24,2048]{2,1,0:T(8,128)(2,1)}), bf16[16,24,2048]{2,1,0:T(8,128)(2,1)}, u32[]{:S(2)}, u32[]{:S(2)}) async-start(bf16[16,24,2048]{2,1,0:T(8,128)(2,1)} %bitcast.40), calls=%async_computation.6 | async-start | bytes 3145728 | tf_op jit(solution)/shard_map/all_to_all | solution.py:281
  114.7 8.8 %copy-start.4 = (bf16[16,24,2048]{2,1,0:T(8,128)(2,1)S(1)}, bf16[16,24,2048]{2,1,0:T(8,128)(2,1)}, u32[]{:S(2)}) copy-start(bf16[16,24,2048]{2,1,0:T(8,128)(2,1)} %copy-done.3) | copy-start | bytes 4718596
  122.3 1.2 copy-start.9
  133.4 1.2 copy-start.5
  136.2 27.4 %all-to-all-start.5 = ((bf16[16,24,2048]{2,1,0:T(8,128)(2,1)}), bf16[16,24,2048]{2,1,0:T(8,128)(2,1)S(1)}, u32[]{:S(2)}, u32[]{:S(2)}) async-start(bf16[16,24,2048]{2,1,0:T(8,128)(2,1)} %bitcast.43), calls=%async_computation.5 | async-start | bytes 3145728 | tf_op jit(solution)/shard_map/all_to_all | solution.py:281
  150.2 1.2 copy-start.10
  151.4 1.1 copy-start.11
  152.5 1.1 copy-start.13
  163.6 27.3 %all-to-all-start.3 = ((bf16[16,24,2048]{2,1,0:T(8,128)(2,1)}), bf16[16,24,2048]{2,1,0:T(8,128)(2,1)}, u32[]{:S(2)}, u32[]{:S(2)}) async-start(bf16[16,24,2048]{2,1,0:T(8,128)(2,1)} %bitcast.46), calls=%async_computation.3 | async-start | bytes 3145728 | tf_op jit(solution)/shard_map/all_to_all | solution.py:281
  170.2 1.3 copy-start.12
  171.4 1.3 copy-start.14
  217.3 32.4 %all-to-all-start.1 = ((bf16[16,24,2048]{2,1,0:T(8,128)(2,1)}), bf16[16,24,2048]{2,1,0:T(8,128)(2,1)S(1)}, u32[]{:S(2)}, u32[]{:S(2)}) async-start(bf16[16,24,2048]{2,1,0:T(8,128)(2,1)} %bitcast.45), calls=%async_computation.1 | async-start | bytes 3145728 | tf_op jit(solution)/shard_map/all_to_all | solution.py:281
  222.3 1.4 copy-start.2
  223.7 6.0 %copy-start.16 = (bf16[128,2048]{1,0:T(8,128)(2,1)S(1)}, bf16[128,2048]{1,0:T(8,128)(2,1)}, u32[]{:S(2)}) copy-start(bf16[128,2048]{1,0:T(8,128)(2,1)} %copy-done.15) | copy-start | bytes 1572868
  224.4 23.9 %collective-permute-start.7 = (bf16[128,2048]{1,0:T(8,128)(2,1)S(1)}, bf16[128,2048]{1,0:T(8,128)(2,1)S(1)}, u32[]{:S(2)}, u32[]{:S(2)}) collective-permute-start(bf16[128,2048]{1,0:T(8,128)(2,1)S(1)} %collect_grad.1), channel_id=1, source_target_pairs={{0,4},{4,0},{1,5},{5,1},{2,6},{6,2},{3,7},{7,3},{8,12},{12,8},{9,1... | collective-permute-start | bytes 1572872 | tf_op jit(solution)/shard_map/ppermute | solution.py:276
  233.0 25.4 %collective-permute-start.5 = (bf16[128,2048]{1,0:T(8,128)(2,1)}, bf16[128,2048]{1,0:T(8,128)(2,1)}, u32[]{:S(2)}, u32[]{:S(2)}) collective-permute-start(bf16[128,2048]{1,0:T(8,128)(2,1)} %get-tuple-element.15), channel_id=1, source_target_pairs={{0,4},{4,0},{1,5},{5,1},{2,6},{6,2},{3,7},{7,3},{8,12},{12,8},{9,1... | collective-permute-start | bytes 1572872 | tf_op jit(solution)/shard_map/ppermute | solution.py:276
  233.7 24.6 %collective-permute-start.6 = (f32[8,128]{1,0:T(8,128)S(1)}, f32[8,128]{1,0:T(8,128)S(1)}, u32[]{:S(2)}, u32[]{:S(2)}) collective-permute-start(f32[8,128]{1,0:T(8,128)S(1)} %get-tuple-element.16), channel_id=1, source_target_pairs={{0,4},{4,0},{1,5},{5,1},{2,6},{6,2},{3,7},{7,3},{8,12},{12,8},{9,1... | collective-permute-start | bytes 12296 | tf_op jit(solution)/shard_map/ppermute | solution.py:276
  258.4 1.0 copy-start.7
  (2 other events, 1.6 us)

commit v2 on v1

--- a/solution.py
+++ b/solution.py
@@ -28,7 +28,7 @@
     return raised / jnp.sum(raised, axis=0, keepdims=True)
 
 
-def row_marks(meta, table, half, rows):
+def row_marks(meta, table, half, rows, stride=CAP, offset=0):
     copies = table.shape[1]
     tokens = meta.shape[1]
     experts = copies - copies // 8
@@ -48,7 +48,7 @@
     hot = second > 0
     target = jnp.where(hot & ((rank & 1) == 1), second, first)
     place = jnp.where(hot, rank >> 1, rank)
-    row = ((target >> 3) * 4 + (target & 3)) * CAP + place
+    row = ((target >> 3) * 4 + (target & 3)) * stride + offset + place
     row = jnp.where(((target >> 2) & 1) == half, row, -1)
     number = lax.broadcasted_iota(jnp.int32, (rows, tokens), 0)
     return [
@@ -64,29 +64,36 @@
     return sum(jnp.where(m, probs[k : k + 1, :], 0.0) for k, m in enumerate(marks))
 
 
-def pack_kernel(half_ref, meta_ref, table_ref, x_ref, out_ref, *, scaled):
-    meta = meta_ref[...]
-    marks = row_marks(meta, table_ref[...], half_ref[0], out_ref.shape[0])
-    picked = dot(either(marks).astype(BF16), x_ref[...], 1, 0)
+def both_marks(own, other, table, half, rows):
+    return [
+        row_marks(meta, table, half, rows, 2 * CAP, i * CAP) for i, meta in enumerate((own, other))
+    ]
+
+
+def pack_kernel(half_ref, meta_ref, meta_other_ref, table_ref, x_ref, x_other_ref, out_ref, *, scaled):
+    metas = meta_ref[...], meta_other_ref[...]
+    marks = both_marks(*metas, table_ref[...], half_ref[0], out_ref.shape[0])
+    onehot = jnp.concatenate([either(m) for m in marks], axis=1).astype(BF16)
+    picked = dot(onehot, jnp.concatenate([x_ref[...], x_other_ref[...]], axis=0), 1, 0)
     if scaled:
-        weight = jnp.sum(weighted(marks, probabilities(meta)), axis=1, keepdims=True)
-        picked = picked * weight
+        probs = [weighted(m, probabilities(meta)) for m, meta in zip(marks, metas)]
+        picked = picked * jnp.sum(probs[0] + probs[1], axis=1, keepdims=True)
     out_ref[...] = picked.astype(BF16)
 
 
-def pack(half, meta, table, x, scaled):
-    rows = 16 * CAP
+def pack(half, meta, meta_other, table, x, x_other, scaled):
+    rows = 32 * CAP
     return pl.pallas_call(
         functools.partial(pack_kernel, scaled=scaled),
         out_shape=jax.ShapeDtypeStruct((rows, x.shape[1]), BF16),
-        in_specs=[SCALAR, ANYWHERE, ANYWHERE, ANYWHERE],
+        in_specs=[SCALAR] + [ANYWHERE] * 5,
         out_specs=ANYWHERE,
         compiler_params=pltpu.CompilerParams(vmem_limit_bytes=VMEM_BYTES),
         cost_estimate=pl.CostEstimate(
-            flops=2 * rows * x.size, bytes_accessed=2 * x.size + 2 * rows * x.shape[1], transcendentals=0
+            flops=4 * rows * x.size, bytes_accessed=4 * x.size + 2 * rows * x.shape[1], transcendentals=0
         ),
         name="pack_grad" if scaled else "pack_in",
-    )(half, meta, table, x)
+    )(half, meta, meta_other, table, x, x_other)
 
 
 def split_dot(weights, rows):
@@ -95,44 +102,62 @@
     return dot(high, rows, 0, 0) + dot(low, rows, 0, 0)
 
 
-def out_kernel(half_ref, meta_ref, table_ref, rows_ref, g_ref, *refs, last):
-    meta = meta_ref[...]
+def out_kernel(
+    half_ref, meta_ref, meta_other_ref, table_ref, rows_ref, g_ref, g_other_ref,
+    own_ref, own_grads_ref, other_ref, other_grads_ref,
+):
+    metas = meta_ref[...], meta_other_ref[...]
     rows = rows_ref[...]
-    marks = row_marks(meta, table_ref[...], half_ref[0], rows.shape[0])
-    probs = probabilities(meta)
-    total = split_dot(weighted(marks, probs), rows)
-    products = dot(rows, g_ref[...], 1, 1)
-    grads = jnp.concatenate(
-        [jnp.sum(jnp.where(m, products, 0.0), axis=0, keepdims=True) for m in marks], axis=0
-    )
-    if last:
-        other_ref, other_grads_ref, out_ref, logit_ref = refs
-        out_ref[...] = (total + other_ref[...].astype(F32)).astype(BF16)
-        grads = grads + other_grads_ref[0:4, :]
-        logit_ref[...] = probs * (grads - jnp.sum(probs * grads, axis=0, keepdims=True))
-    else:
-        out_ref, grads_ref = refs
-        out_ref[...] = total.astype(BF16)
-        grads_ref[...] = jnp.concatenate([grads, jnp.zeros_like(grads)], axis=0)
-
-
-def collect_out(half, meta, table, rows, g, other=None):
-    last = other is not None
-    extra = list(other) if last else []
-    return pl.pallas_call(
-        functools.partial(out_kernel, last=last),
+    marks = both_marks(*metas, table_ref[...], half_ref[0], rows.shape[0])
+    weights = [weighted(m, probabilities(meta)) for m, meta in zip(marks, metas)]
+    own_ref[...] = split_dot(weights[0], rows)
+    other_ref[...] = split_dot(weights[1], rows).astype(BF16)
+    for ref, m, grads in zip((own_grads_ref, other_grads_ref), marks, (g_ref, g_other_ref)):
+        products = dot(rows, grads[...], 1, 1)
+        sums = [jnp.sum(jnp.where(k, products, 0.0), axis=0, keepdims=True) for k in m]
+        ref[...] = jnp.concatenate(sums + [jnp.zeros_like(s) for s in sums], axis=0)
+
+
+def collect_out(half, meta, meta_other, table, rows, g, g_other):
+    sums = jax.ShapeDtypeStruct((8, g.shape[0]), F32)
+    return pl.pallas_call(
+        out_kernel,
         out_shape=(
+            jax.ShapeDtypeStruct(g.shape, F32),
+            sums,
             jax.ShapeDtypeStruct(g.shape, BF16),
-            jax.ShapeDtypeStruct((4 if last else 8, g.shape[0]), F32),
-        ),
-        in_specs=[SCALAR] + [ANYWHERE] * (4 + len(extra)),
+            sums,
+        ),
+        in_specs=[SCALAR] + [ANYWHERE] * 6,
+        out_specs=(ANYWHERE,) * 4,
+        compiler_params=pltpu.CompilerParams(vmem_limit_bytes=VMEM_BYTES),
+        cost_estimate=pl.CostEstimate(
+            flops=12 * rows.shape[0] * g.size, bytes_accessed=2 * rows.size + 12 * g.size, transcendentals=0
+        ),
+        name="collect_out",
+    )(half, meta, meta_other, table, rows, g, g_other)
+
+
+def finish_kernel(meta_ref, own_ref, own_grads_ref, other_ref, other_grads_ref, out_ref, logit_ref):
+    out_ref[...] = (own_ref[...] + other_ref[...].astype(F32)).astype(BF16)
+    probs = probabilities(meta_ref[...])
+    grads = own_grads_ref[0:4, :] + other_grads_ref[0:4, :]
+    logit_ref[...] = probs * (grads - jnp.sum(probs * grads, axis=0, keepdims=True))
+
+
+def finish_out(meta, own, own_grads, other, other_grads):
+    return pl.pallas_call(
+        finish_kernel,
+        out_shape=(
+            jax.ShapeDtypeStruct(own.shape, BF16),
+            jax.ShapeDtypeStruct((4, own.shape[0]), F32),
+        ),
+        in_specs=[ANYWHERE] * 5,
         out_specs=(ANYWHERE, ANYWHERE),
         compiler_params=pltpu.CompilerParams(vmem_limit_bytes=VMEM_BYTES),
-        cost_estimate=pl.CostEstimate(
-            flops=6 * rows.shape[0] * g.size, bytes_accessed=2 * rows.size + 4 * g.size, transcendentals=0
-        ),
-        name="collect_out_last" if last else "collect_out",
-    )(half, meta, table, rows, g, *extra)
+        cost_estimate=pl.CostEstimate(flops=2 * own.size, bytes_accessed=8 * own.size, transcendentals=0),
+        name="finish_out",
+    )(meta, own, own_grads, other, other_grads)
 
 
 def grad_kernel(half_ref, meta_ref, table_ref, rows_ref, *refs, last):
@@ -184,7 +209,7 @@
         out_ref[...] = total[...].astype(BF16)
 
 
-def backward_kernel(g_ref, gate_ref, up_ref, wg_ref, wu_ref, wd_ref, out_ref, total):
+def backward_kernel(g_ref, gate_ref, up_ref, wg_ref, wu_ref, wd_ref, own_ref, other_ref, total):
     step = pl.program_id(0)
     hidden_grad = dot(g_ref[...], wd_ref[...], 1, 1)
     gate = gate_ref[...]
@@ -204,7 +229,9 @@
 
     @pl.when(step == pl.num_programs(0) - 1)
     def _():
-        out_ref[...] = total[...].astype(BF16)
+        for i in range(own_ref.shape[0]):
+            own_ref[i] = total[2 * CAP * i : 2 * CAP * i + CAP, :].astype(BF16)
+            other_ref[i] = total[2 * CAP * i + CAP : 2 * CAP * (i + 1), :].astype(BF16)
 
 
 BLOCK = 256
@@ -253,12 +280,13 @@
     rows, width = g.shape
     hidden = w_dn.shape[0]
     steps, whole, gate, up, down, pre = expert_specs(rows, width, hidden)
+    block = (rows // (2 * CAP), CAP, width)
     return pl.pallas_call(
         backward_kernel,
         grid=(steps,),
-        out_shape=jax.ShapeDtypeStruct((rows, width), BF16),
+        out_shape=(jax.ShapeDtypeStruct(block, BF16),) * 2,
         in_specs=[whole, pre, pre, gate, up, down],
-        out_specs=whole,
+        out_specs=(pl.BlockSpec(block, lambda j: (0, 0, 0)),) * 2,
         scratch_shapes=[pltpu.VMEM((rows, width), F32)],
         compiler_params=pltpu.CompilerParams(vmem_limit_bytes=VMEM_BYTES),
         cost_estimate=expert_cost(rows, width, hidden),
@@ -266,58 +294,62 @@
     )(g, gates, ups, w_gu, w_gu, w_dn)
 
 
-def passed_along(x, by):
-    devices = SIZES[0] * SIZES[1]
-    pairs = [(i, i + by) for i in range(devices) if 0 <= i + by < devices]
-    return lax.ppermute(x, SECTION, pairs)
-
-
-def swapped(x):
-    return lax.ppermute(x, "z_hi", [(0, 1), (1, 0)])
+def after(x, *earlier):
+    return lax.optimization_barrier((x, *earlier))[0]
+
+
+def shifted(x, by):
+    sections = SIZES[0] * SIZES[1]
+    pairs = [(i, i + by) for i in range(sections) if 0 <= i + by < sections]
+    here = lax.axis_index(SECTION) == (0 if by > 0 else sections - 1)
+    return jnp.where(here, x, lax.ppermute(x, SECTION, pairs))
+
+
+def swapped(x, cores=(0, 1)):
+    pairs = [(2 * c + h, 2 * c + 1 - h) for c in cores for h in range(2)]
+    return lax.ppermute(x, ("core", "z_hi"), pairs)
 
 
 def exchanged(rows):
     width = rows.shape[-1]
     moved = lax.all_to_all(
-        rows.reshape(16, CAP, width), PLANE, split_axis=0, concat_axis=0, tiled=True
-    )
-    return moved.reshape(16 * CAP, width)
+        rows.reshape(16, -1, width), PLANE, split_axis=0, concat_axis=0, tiled=True
+    )
+    return moved.reshape(-1, width)
 
 
 def local(x_held, grad_held, expert_ids, gate_logits, placement, w_gate_up, w_down):
-    own_x = x_held[0]
-    own_g = grad_held[0]
     w_gu = w_gate_up[0, 0]
     w_dn = w_down[0, 0]
-    section = lax.axis_index(SECTION)
-    sections = SIZES[0] * SIZES[1]
     half = lax.axis_index("z_hi").astype(jnp.int32).reshape(1)
     table = placement
 
     meta = jnp.concatenate([expert_ids[0].astype(F32).T, gate_logits[0].T], axis=0)
     meta_other = swapped(meta)
-    x = jnp.where(section == 0, own_x, passed_along(own_x, 1))
-    g = jnp.where(section == sections - 1, own_g, passed_along(own_g, -1))
-    x_other = swapped(x)
-    g_other = swapped(g)
-
-    x_rows = exchanged(pack(half, meta, table, x, False))
-    x_rows_other = exchanged(pack(half, meta_other, table, x_other, False))
-    g_rows = exchanged(pack(half, meta, table, g, True))
-    g_rows_other = exchanged(pack(half, meta_other, table, g_other, True))
-
+    odd = lax.axis_index("core") == 1
+    x_odd = lax.ppermute(
+        x_held[0],
+        SECTION + ("z_hi",),
+        [(4 * i + h, 4 * i + 3 - h) for i in range(SIZES[0]) for h in range(2)],
+    )
+    x = shifted(x_held[0], 1)
+    g = shifted(grad_held[0], -1)
+    x_even = swapped(after(x, g), (0,))
+    x_other = jnp.where(odd, x_odd, x_even)
+    packed = pack(half, meta, meta_other, table, x, x_other, False)
+    x_rows = exchanged(packed)
+    g_other = swapped(after(g, packed))
+    g_rows = exchanged(after(pack(half, meta, meta_other, table, g, g_other, True), x_rows))
     out, gate, up = expert_forward(x_rows, w_gu, w_dn)
-    out_other, gate_other, up_other = expert_forward(x_rows_other, w_gu, w_dn)
-    out_other = exchanged(out_other)
-    out = exchanged(out)
-    back_other = exchanged(expert_backward(g_rows_other, gate_other, up_other, w_gu, w_dn))
-    back = exchanged(expert_backward(g_rows, gate, up, w_gu, w_dn))
-
-    part, part_grads = collect_out(half, meta_other, table, out_other, g_other)
-    part = swapped(part)
-    part_grads = swapped(part_grads)
+    out = exchanged(after(out, g_rows))
+    back, back_other = expert_backward(g_rows, gate, up, w_gu, w_dn)
+    back_other = exchanged(after(back_other, out))
+
+    own, own_grads, other, other_grads = collect_out(half, meta, meta_other, table, out, g, g_other)
+    other, other_grads = swapped(other), swapped(other_grads)
+    back = exchanged(after(back, back_other, other, other_grads))
+    section_out, logit_grad = finish_out(meta, own, own_grads, other, other_grads)
     back_part = swapped(collect_grad(half, meta_other, table, back_other))
-    section_out, logit_grad = collect_out(half, meta, table, out, g, (part, part_grads))
     input_grad = collect_grad(half, meta, table, back, back_part)
     return section_out[None], input_grad[None], logit_grad.T[None]
 

time: 264 us -> 243 us (0.920)
  the two profiles are of different devices: /device:TPU:66 before, /device:TPU:1 now
where the time goes in v2:
time: 243 us
  waiting for transfers between devices  95.2 us (39%)
  starting transfers between devices  80.9 us (33%)
  Pallas kernels  46.5 us (19%)
  local copies, waits for them, and re-layouts  16.9 us (7%)
    all_to_all x5, waiting for transfers between devices, exchanged(): lax.all_to_all(rows.reshape(16, -1, width), PLANE, split_axis=0, concat_a...  55.5 us
    ppermute x6, starting transfers between devices, swapped(): return lax.ppermute(x, ('core', 'z_hi'), pairs)  44.2 us
    ppermute x6, waiting for transfers between devices, swapped(): return lax.ppermute(x, ('core', 'z_hi'), pairs)  34.4 us
    all_to_all x5, starting transfers between devices, exchanged(): lax.all_to_all(rows.reshape(16, -1, width), PLANE, split_axis=0, concat_a...  28.1 us
    pallas_call x1, Pallas kernels, expert_backward(): pl.pallas_call(backward_kernel, grid=(steps,), out_shape=(jax.ShapeDtypeS...  18.1 us
    unnamed x38, local copies, waits for them, and re-layouts  16.9 us
    pallas_call x1, Pallas kernels, expert_forward(): pl.pallas_call(forward_kernel, grid=(steps,), out_shape=(jax.ShapeDtypeSt...  14.9 us
    ppermute x2, starting transfers between devices, shifted(): return jnp.where(here, x, lax.ppermute(x, SECTION, pairs))  7.2 us
  transfers between devices with their start and end apart: 14, of which 10 were waited for; matrix products, arithmetic and copies ran while one was open for 1% of the time, Pallas kernels for 17%

profile of v2, /device:TPU:1, one launch (start us, length us, event | category | flops | bytes accessed | tf_op | source)
XLA Modules:
  0.0 242.7 jit_solution(128335538306876705)
XLA Ops:
  0.7 5.3 %collective-permute-start.3 = (bf16[128,2048]{1,0:T(8,128)(2,1)}, bf16[128,2048]{1,0:T(8,128)(2,1)S(1)}, u32[]{:S(2)}, u32[]{:S(2)}) collective-permute-start(bf16[128,2048]{1,0:T(8,128)(2,1)} %bitcast.33), channel_id=1, source_target_pairs={{32,0},{64,32},{96,64},{128,96},{160,128},{192,160},{224,192},{33,... | collective-permute-start | bytes 1572872 | tf_op jit(solution)/shard_map/ppermute | solution.py:305
  5.9 1.9 collective-permute-start.1
  7.9 1.3 collective-permute-start.2
  9.2 3.6 %collective-permute-done.3 = bf16[128,2048]{1,0:T(8,128)(2,1)S(1)} collective-permute-done((bf16[128,2048]{1,0:T(8,128)(2,1)}, bf16[128,2048]{1,0:T(8,128)(2,1)S(1)}, u32[]{:S(2)}, u32[]{:S(2)}) %collective-permute-start.3) | collective-permute-done | bytes 524320 | tf_op jit(solution)/shard_map/ppermute | solution.py:305
  16.2 11.8 %collective-permute-start = (f32[8,128]{1,0:T(8,128)S(1)}, f32[8,128]{1,0:T(8,128)S(1)}, u32[]{:S(2)}, u32[]{:S(2)}) collective-permute-start(f32[8,128]{1,0:T(8,128)S(1)} %pad_maximum_fusion.meta_ref), channel_id=1, source_target_pairs={{0,4},{4,0},{32,36},{36,32},{1,5},{5,1},{33,37},{37,33},{2,6},{6,2... | collective-permute-start | bytes 12296 | tf_op jit(solution)/shard_map/ppermute | solution.py:310
  28.0 1.4 collective-permute-done.2
  29.5 2.9 %pack_in.1 = bf16[768,2048]{1,0:T(8,128)(2,1)} custom-call(s32[1]{0:T(128)} %bitcast.4.half_ref, f32[8,128]{1,0:T(8,128)S(1)} %pad_maximum_fusion.meta_ref, f32[8,128]{1,0:T(8,128)S(1)} %collective-permute-done.meta_other_ref.meta_ref, s32[1,32]{1,0:T(1,128)S(1)} %copy-done.12, bf16[128,2048]{1,0:T(8,128)(2,1)S(1)} %broadcast_select_fusion.2.x_ref, ...), custom_call_target="tpu_custom_call" | custom-call | flops 805306368 | bytes 4194304 | tf_op jit(solution)/shard_map/pack_in/pallas_call | solution.py:86
  32.4 7.1 %all-to-all-start = ((bf16[16,48,2048]{2,1,0:T(8,128)(2,1)}), bf16[16,48,2048]{2,1,0:T(8,128)(2,1)}, u32[]{:S(2)}, u32[]{:S(2)}) async-start(bf16[16,48,2048]{2,1,0:T(8,128)(2,1)} %bitcast.7), calls=%async_computation | async-start | bytes 6291456 | tf_op jit(solution)/shard_map/all_to_all | solution.py:315
  39.5 5.5 %collective-permute-start.5 = (bf16[128,2048]{1,0:T(8,128)(2,1)S(1)}, bf16[128,2048]{1,0:T(8,128)(2,1)S(1)}, u32[]{:S(2)}, u32[]{:S(2)}) collective-permute-start(bf16[128,2048]{1,0:T(8,128)(2,1)S(1)} %broadcast_select_fusion.x_ref.g_ref), channel_id=1, source_target_pairs={{0,4},{4,0},{32,36},{36,32},{1,5},{5,1},{33,37},{37,33},{2,6},{6,2... | collective-permute-start | bytes 1572872 | tf_op jit(solution)/shard_map/ppermute | solution.py:310
  44.9 6.6 %collective-permute-done.5.x_other_ref.g_other_ref = bf16[128,2048]{1,0:T(8,128)(2,1)S(1)} collective-permute-done((bf16[128,2048]{1,0:T(8,128)(2,1)S(1)}, bf16[128,2048]{1,0:T(8,128)(2,1)S(1)}, u32[]{:S(2)}, u32[]{:S(2)}) %collective-permute-start.5) | collective-permute-done | bytes 524320 | tf_op jit(solution)/shard_map/ppermute | solution.py:310
  51.5 3.2 %pack_grad.1 = bf16[768,2048]{1,0:T(8,128)(2,1)} custom-call(s32[1]{0:T(128)} %bitcast.4.half_ref, f32[8,128]{1,0:T(8,128)S(1)} %pad_maximum_fusion.meta_ref, f32[8,128]{1,0:T(8,128)S(1)} %collective-permute-done.meta_other_ref.meta_ref, s32[1,32]{1,0:T(1,128)S(1)} %copy-done.12, bf16[128,2048]{1,0:T(8,128)(2,1)S(1)} %broadcast_select_fusion.x_ref.g_ref, ...), custom_call_target="tpu_custom_call" | custom-call | flops 805306368 | bytes 4194304 | tf_op jit(solution)/shard_map/pack_grad/pallas_call | solution.py:86
  55.6 19.2 %all-to-all-done = bf16[16,48,2048]{2,1,0:T(8,128)(2,1)} async-done(((bf16[16,48,2048]{2,1,0:T(8,128)(2,1)}), bf16[16,48,2048]{2,1,0:T(8,128)(2,1)}, u32[]{:S(2)}, u32[]{:S(2)}) %all-to-all-start) | async-done | bytes 3145760 | tf_op jit(solution)/shard_map/all_to_all | solution.py:315
  74.8 4.8 %all-to-all-start.1 = ((bf16[16,48,2048]{2,1,0:T(8,128)(2,1)}), bf16[16,48,2048]{2,1,0:T(8,128)(2,1)S(1)}, u32[]{:S(2)}, u32[]{:S(2)}) async-start(bf16[16,48,2048]{2,1,0:T(8,128)(2,1)} %bitcast.11), calls=%async_computation.1 | async-start | bytes 6291456 | tf_op jit(solution)/shard_map/all_to_all | solution.py:315
  79.6 14.9 %expert_forward.1 = (bf16[768,2048]{1,0:T(8,128)(2,1)}, f32[768,768]{1,0:T(8,128)S(1)}, f32[768,768]{1,0:T(8,128)S(1)}) custom-call(bf16[768,2048]{1,0:T(8,128)(2,1)} %bitcast.8.x_ref, bf16[2048,1536]{1,0:T(8,128)(2,1)} %bitcast.37, bf16[2048,1536]{1,0:T(8,128)(2,1)} %bitcast.38, bf16[768,2048]{1,0:T(8,128)(2,1)} %bitcast.41), custom_call_target="tpu_custom_call" | custom-call | flops 7247757312 | bytes 20447232 | tf_op jit(solution)/shard_map/expert_forward/pallas_call | solution.py:262
  94.5 1.4 copy-done.13
  96.0 1.4 copy-done.15
  97.4 17.4 %all-to-all-done.1 = bf16[16,48,2048]{2,1,0:T(8,128)(2,1)S(1)} async-done(((bf16[16,48,2048]{2,1,0:T(8,128)(2,1)}), bf16[16,48,2048]{2,1,0:T(8,128)(2,1)S(1)}, u32[]{:S(2)}, u32[]{:S(2)}) %all-to-all-start.1) | async-done | bytes 3145760 | tf_op jit(solution)/shard_map/all_to_all | solution.py:315
  114.8 1.7 copy-done.16
  116.5 4.6 %all-to-all-start.2 = ((bf16[16,48,2048]{2,1,0:T(8,128)(2,1)}), bf16[16,48,2048]{2,1,0:T(8,128)(2,1)S(1)}, u32[]{:S(2)}, u32[]{:S(2)}) async-start(bf16[16,48,2048]{2,1,0:T(8,128)(2,1)} %bitcast.31), calls=%async_computation.2 | async-start | bytes 6291456 | tf_op jit(solution)/shard_map/all_to_all | solution.py:315
  121.1 1.7 copy-done.14
  122.7 18.1 %expert_backward.1 = (bf16[16,24,2048]{2,1,0:T(8,128)(2,1)S(1)}, bf16[16,24,2048]{2,1,0:T(8,128)(2,1)S(1)}) custom-call(bf16[768,2048]{1,0:T(8,128)(2,1)} %bitcast.30, f32[768,768]{1,0:T(8,128)S(1)} %copy-done.14, f32[768,768]{1,0:T(8,128)} %copy-done.15, bf16[2048,1536]{1,0:T(8,128)(2,1)} %bitcast.39, bf16[2048,1536]{1,0:T(8,128)(2,1)} %bitcast.40, ...), custom_call_target="tpu_custom_call" | custom-call | flops 7247757312 | bytes 20447232 | tf_op jit(solution)/shard_map/expert_backward/pallas_call | solution.py:284
  143.1 13.2 %all-to-all-done.2 = bf16[16,48,2048]{2,1,0:T(8,128)(2,1)S(1)} async-done(((bf16[16,48,2048]{2,1,0:T(8,128)(2,1)}), bf16[16,48,2048]{2,1,0:T(8,128)(2,1)S(1)}, u32[]{:S(2)}, u32[]{:S(2)}) %all-to-all-start.2) | async-done | bytes 3145760 | tf_op jit(solution)/shard_map/all_to_all | solution.py:315
  156.3 1.6 copy-done
  158.0 4.8 %all-to-all-start.3 = ((bf16[16,24,2048]{2,1,0:T(8,128)(2,1)}), bf16[16,24,2048]{2,1,0:T(8,128)(2,1)S(1)}, u32[]{:S(2)}, u32[]{:S(2)}) async-start(bf16[16,24,2048]{2,1,0:T(8,128)(2,1)} %copy-done.5), calls=%async_computation.3 | async-start | bytes 3145728 | tf_op jit(solution)/shard_map/all_to_all | solution.py:315
  162.9 1.9 copy-done.1
  164.7 4.3 %collect_out.1 = (f32[128,2048]{1,0:T(8,128)S(1)}, f32[8,128]{1,0:T(8,128)S(1)}, bf16[128,2048]{1,0:T(8,128)(2,1)S(1)}, f32[8,128]{1,0:T(8,128)S(1)}) custom-call(s32[1]{0:T(128)} %bitcast.4.half_ref, f32[8,128]{1,0:T(8,128)S(1)} %pad_maximum_fusion.meta_ref, f32[8,128]{1,0:T(8,128)S(1)} %collective-permute-done.meta_other_ref.meta_ref, ...), custom_call_target="tpu_custom_call" | custom-call | flops 2415919104 | bytes 6291456 | tf_op jit(solution)/shard_map/collect_out/pallas_call | solution.py:123
  170.0 26.2 %collective-permute-start.6 = (bf16[128,2048]{1,0:T(8,128)(2,1)S(1)}, bf16[128,2048]{1,0:T(8,128)(2,1)S(1)}, u32[]{:S(2)}, u32[]{:S(2)}) collective-permute-start(bf16[128,2048]{1,0:T(8,128)(2,1)S(1)} %get-tuple-element.27), channel_id=1, source_target_pairs={{0,4},{4,0},{32,36},{36,32},{1,5},{5,1},{33,37},{37,33},{2,6},{6,2... | collective-permute-start | bytes 1572872 | tf_op jit(solution)/shard_map/ppermute | solution.py:310
  196.2 14.6 %collective-permute-done.7.other_grads_ref = f32[8,128]{1,0:T(8,128)S(1)} collective-permute-done((f32[8,128]{1,0:T(8,128)S(1)}, f32[8,128]{1,0:T(8,128)S(1)}, u32[]{:S(2)}, u32[]{:S(2)}) %collective-permute-start.7) | collective-permute-done | bytes 4128 | tf_op jit(solution)/shard_map/ppermute | solution.py:310
  211.6 6.9 %all-to-all-start.4 = ((bf16[16,24,2048]{2,1,0:T(8,128)(2,1)}), bf16[16,24,2048]{2,1,0:T(8,128)(2,1)S(1)}, u32[]{:S(2)}, u32[]{:S(2)}) async-start(bf16[16,24,2048]{2,1,0:T(8,128)(2,1)} %copy-done.4), calls=%async_computation.4 | async-start | bytes 3145728 | tf_op jit(solution)/shard_map/all_to_all | solution.py:315
  222.5 13.1 %collective-permute-done.8.refs_0_ = bf16[128,2048]{1,0:T(8,128)(2,1)S(1)} collective-permute-done((bf16[128,2048]{1,0:T(8,128)(2,1)S(1)}, bf16[128,2048]{1,0:T(8,128)(2,1)S(1)}, u32[]{:S(2)}, u32[]{:S(2)}) %collective-permute-start.8) | collective-permute-done | bytes 524320 | tf_op jit(solution)/shard_map/ppermute | solution.py:310
  235.6 5.6 %all-to-all-done.4 = bf16[16,24,2048]{2,1,0:T(8,128)(2,1)S(1)} async-done(((bf16[16,24,2048]{2,1,0:T(8,128)(2,1)}), bf16[16,24,2048]{2,1,0:T(8,128)(2,1)S(1)}, u32[]{:S(2)}, u32[]{:S(2)}) %all-to-all-start.4) | async-done | bytes 1572896 | tf_op jit(solution)/shard_map/all_to_all | solution.py:315
  241.2 1.5 collect_grad_last.1
  (47 shorter events, 12.3 us)
Async XLA Ops:
  0.6 15.5 %copy-start.17 = (s32[1,128,4]{1,2,0:T(4,128)S(1)}, s32[1,128,4]{1,2,0:T(4,128)}, u32[]{:S(2)}) copy-start(s32[1,128,4]{1,2,0:T(4,128)} %param.9) | copy-start | bytes 6148
  0.6 15.5 %copy-start.18 = (f32[1,128,4]{1,2,0:T(4,128)S(1)}, f32[1,128,4]{1,2,0:T(4,128)}, u32[]{:S(2)}) copy-start(f32[1,128,4]{1,2,0:T(4,128)} %param.10) | copy-start | bytes 6148
  0.7 28.8 %copy-start.12 = (s32[1,32]{1,0:T(1,128)S(1)}, s32[1,32]{1,0:T(1,128)}, u32[]{:S(2)}) copy-start(s32[1,32]{1,0:T(1,128)} %table_ref.9) | copy-start | bytes 388
  0.7 12.1 %collective-permute-start.3 = (bf16[128,2048]{1,0:T(8,128)(2,1)}, bf16[128,2048]{1,0:T(8,128)(2,1)S(1)}, u32[]{:S(2)}, u32[]{:S(2)}) collective-permute-start(bf16[128,2048]{1,0:T(8,128)(2,1)} %bitcast.33), channel_id=1, source_target_pairs={{32,0},{64,32},{96,64},{128,96},{160,128},{192,160},{224,192},{33,... | collective-permute-start | bytes 1572872 | tf_op jit(solution)/shard_map/ppermute | solution.py:305
  5.9 8.3 %collective-permute-start.1 = (bf16[128,2048]{1,0:T(8,128)(2,1)}, bf16[128,2048]{1,0:T(8,128)(2,1)S(1)}, u32[]{:S(2)}, u32[]{:S(2)}) collective-permute-start(bf16[128,2048]{1,0:T(8,128)(2,1)} %bitcast.34), channel_id=1, source_target_pairs={{0,32},{32,64},{64,96},{96,128},{128,160},{160,192},{192,224},{1,3... | collective-permute-start | bytes 1572872 | tf_op jit(solution)/shard_map/ppermute | solution.py:305
  7.9 21.5 %collective-permute-start.2 = (bf16[128,2048]{1,0:T(8,128)(2,1)}, bf16[128,2048]{1,0:T(8,128)(2,1)S(1)}, u32[]{:S(2)}, u32[]{:S(2)}) collective-permute-start(bf16[128,2048]{1,0:T(8,128)(2,1)} %bitcast.35), channel_id=1, source_target_pairs={{0,36},{4,32},{64,100},{68,96},{128,164},{132,160},{192,228},{196,... | collective-permute-start | bytes 1572872 | tf_op jit(solution)/shard_map/ppermute | solution.py:330
  13.9 37.6 %copy-start.2 = (bf16[128,2048]{1,0:T(8,128)(2,1)}, bf16[128,2048]{1,0:T(8,128)(2,1)S(1)}, u32[]{:S(2)}) copy-start(bf16[128,2048]{1,0:T(8,128)(2,1)S(1)} %broadcast_select_fusion.x_ref.g_ref) | copy-start | bytes 1572868
  15.4 14.0 %collective-permute-start.4 = (bf16[128,2048]{1,0:T(8,128)(2,1)S(1)}, bf16[128,2048]{1,0:T(8,128)(2,1)S(1)}, u32[]{:S(2)}, u32[]{:S(2)}) collective-permute-start(bf16[128,2048]{1,0:T(8,128)(2,1)S(1)} %broadcast_select_fusion.2.x_ref), channel_id=1, source_target_pairs={{0,4},{4,0},{1,5},{5,1},{2,6},{6,2},{3,7},{7,3},{8,12},{12,8},{9,1... | collective-permute-start | bytes 1572872 | tf_op jit(solution)/shard_map/ppermute | solution.py:310
  16.2 13.3 %collective-permute-start = (f32[8,128]{1,0:T(8,128)S(1)}, f32[8,128]{1,0:T(8,128)S(1)}, u32[]{:S(2)}, u32[]{:S(2)}) collective-permute-start(f32[8,128]{1,0:T(8,128)S(1)} %pad_maximum_fusion.meta_ref), channel_id=1, source_target_pairs={{0,4},{4,0},{32,36},{36,32},{1,5},{5,1},{33,37},{37,33},{2,6},{6,2... | collective-permute-start | bytes 12296 | tf_op jit(solution)/shard_map/ppermute | solution.py:310
  32.4 42.4 %all-to-all-start = ((bf16[16,48,2048]{2,1,0:T(8,128)(2,1)}), bf16[16,48,2048]{2,1,0:T(8,128)(2,1)}, u32[]{:S(2)}, u32[]{:S(2)}) async-start(bf16[16,48,2048]{2,1,0:T(8,128)(2,1)} %bitcast.7), calls=%async_computation | async-start | bytes 6291456 | tf_op jit(solution)/shard_map/all_to_all | solution.py:315
  39.5 12.1 %collective-permute-start.5 = (bf16[128,2048]{1,0:T(8,128)(2,1)S(1)}, bf16[128,2048]{1,0:T(8,128)(2,1)S(1)}, u32[]{:S(2)}, u32[]{:S(2)}) collective-permute-start(bf16[128,2048]{1,0:T(8,128)(2,1)S(1)} %broadcast_select_fusion.x_ref.g_ref), channel_id=1, source_target_pairs={{0,4},{4,0},{32,36},{36,32},{1,5},{5,1},{33,37},{37,33},{2,6},{6,2... | collective-permute-start | bytes 1572872 | tf_op jit(solution)/shard_map/ppermute | solution.py:310
  74.8 40.0 %all-to-all-start.1 = ((bf16[16,48,2048]{2,1,0:T(8,128)(2,1)}), bf16[16,48,2048]{2,1,0:T(8,128)(2,1)S(1)}, u32[]{:S(2)}, u32[]{:S(2)}) async-start(bf16[16,48,2048]{2,1,0:T(8,128)(2,1)} %bitcast.11), calls=%async_computation.1 | async-start | bytes 6291456 | tf_op jit(solution)/shard_map/all_to_all | solution.py:315
  94.5 1.5 copy-start.13
  96.0 1.4 copy-start.15
  114.8 1.7 copy-start.16
  116.5 39.9 %all-to-all-start.2 = ((bf16[16,48,2048]{2,1,0:T(8,128)(2,1)}), bf16[16,48,2048]{2,1,0:T(8,128)(2,1)S(1)}, u32[]{:S(2)}, u32[]{:S(2)}) async-start(bf16[16,48,2048]{2,1,0:T(8,128)(2,1)} %bitcast.31), calls=%async_computation.2 | async-start | bytes 6291456 | tf_op jit(solution)/shard_map/all_to_all | solution.py:315
  121.0 1.7 copy-start.14
  140.8 1.1 copy-start.4
  141.9 1.2 copy-start.5
  156.3 1.6 copy-start
  158.0 4.8 %copy-start.3 = (bf16[128,2048]{1,0:T(8,128)(2,1)S(1)}, bf16[128,2048]{1,0:T(8,128)(2,1)}, u32[]{:S(2)}) copy-start(bf16[128,2048]{1,0:T(8,128)(2,1)} %copy-done.2) | copy-start | bytes 1572868
  158.0 4.9 %copy-start.9 = (bf16[128,2048]{1,0:T(8,128)(2,1)S(1)}, bf16[128,2048]{1,0:T(8,128)(2,1)}, u32[]{:S(2)}) copy-start(bf16[128,2048]{1,0:T(8,128)(2,1)} %copy-done.8) | copy-start | bytes 1572868
  158.0 53.6 %all-to-all-start.3 = ((bf16[16,24,2048]{2,1,0:T(8,128)(2,1)}), bf16[16,24,2048]{2,1,0:T(8,128)(2,1)S(1)}, u32[]{:S(2)}, u32[]{:S(2)}) async-start(bf16[16,24,2048]{2,1,0:T(8,128)(2,1)} %copy-done.5), calls=%async_computation.3 | async-start | bytes 3145728 | tf_op jit(solution)/shard_map/all_to_all | solution.py:315
  162.8 1.9 copy-start.1
  169.0 1.0 copy-start.6
  170.0 40.8 %collective-permute-start.6 = (bf16[128,2048]{1,0:T(8,128)(2,1)S(1)}, bf16[128,2048]{1,0:T(8,128)(2,1)S(1)}, u32[]{:S(2)}, u32[]{:S(2)}) collective-permute-start(bf16[128,2048]{1,0:T(8,128)(2,1)S(1)} %get-tuple-element.27), channel_id=1, source_target_pairs={{0,4},{4,0},{32,36},{36,32},{1,5},{5,1},{33,37},{37,33},{2,6},{6,2... | collective-permute-start | bytes 1572872 | tf_op jit(solution)/shard_map/ppermute | solution.py:310
  196.2 14.6 %collective-permute-start.7 = (f32[8,128]{1,0:T(8,128)S(1)}, f32[8,128]{1,0:T(8,128)S(1)}, u32[]{:S(2)}, u32[]{:S(2)}) collective-permute-start(f32[8,128]{1,0:T(8,128)S(1)} %get-tuple-element.28), channel_id=1, source_target_pairs={{0,4},{4,0},{32,36},{36,32},{1,5},{5,1},{33,37},{37,33},{2,6},{6,2... | collective-permute-start | bytes 12296 | tf_op jit(solution)/shard_map/ppermute | solution.py:310
  210.8 0.8 copy-start.10
  211.6 29.6 %all-to-all-start.4 = ((bf16[16,24,2048]{2,1,0:T(8,128)(2,1)}), bf16[16,24,2048]{2,1,0:T(8,128)(2,1)S(1)}, u32[]{:S(2)}, u32[]{:S(2)}) async-start(bf16[16,24,2048]{2,1,0:T(8,128)(2,1)} %copy-done.4), calls=%async_computation.4 | async-start | bytes 3145728 | tf_op jit(solution)/shard_map/all_to_all | solution.py:315
  219.2 16.4 %collective-permute-start.8 = (bf16[128,2048]{1,0:T(8,128)(2,1)S(1)}, bf16[128,2048]{1,0:T(8,128)(2,1)S(1)}, u32[]{:S(2)}, u32[]{:S(2)}) collective-permute-start(bf16[128,2048]{1,0:T(8,128)(2,1)S(1)} %collect_grad.1), channel_id=1, source_target_pairs={{0,4},{4,0},{32,36},{36,32},{1,5},{5,1},{33,37},{37,33},{2,6},{6,2... | collective-permute-start | bytes 1572872 | tf_op jit(solution)/shard_map/ppermute | solution.py:310
  219.3 1.2 copy-start.7
  220.5 1.0 copy-start.11
  (1 other events, 0.8 us)

commit v3 on v1

v3 whole, which is shorter than its diff:
```python
import functools

import jax
import jax.numpy as jnp
from jax import lax
from jax.experimental import pallas as pl
from jax.experimental.pallas import tpu as pltpu
from jax.sharding import Mesh, PartitionSpec as P

F32 = jnp.float32
BF16 = jnp.bfloat16
SECTION = ("z_lo", "core")
EXPERT = ("y", "z_hi", "x")
PLANE = ("y", "x")
SIZES = (4, 2, 4, 2, 4)
CAP = 24
VMEM_BYTES = 48 * 1024 * 1024
ANYWHERE = pl.BlockSpec(memory_space=pltpu.VMEM)
SCALAR = pl.BlockSpec(memory_space=pltpu.SMEM)


def dot(a, b, ca, cb):
    return lax.dot_general(a, b, (((ca,), (cb,)), ((), ())), preferred_element_type=F32)


def probabilities(meta):
    raised = jnp.exp(meta[4:8, :])
    return raised / jnp.sum(raised, axis=0, keepdims=True)


def row_marks(meta, table, half, rows):
    copies = table.shape[1]
    tokens = meta.shape[1]
    experts = copies - copies // 8
    ids = meta[0:4, :].astype(jnp.int32)
    label = lax.broadcasted_iota(jnp.int32, (copies, tokens), 0)
    named = [ids[k : k + 1, :] == label for k in range(4)]
    onehot = sum(n.astype(F32) for n in named).astype(BF16)
    earlier = (
        lax.broadcasted_iota(jnp.int32, (tokens, tokens), 0)
        < lax.broadcasted_iota(jnp.int32, (tokens, tokens), 1)
    ).astype(F32).astype(BF16)
    rank = dot(onehot, earlier, 1, 0).astype(jnp.int32)
    copy = lax.broadcasted_iota(jnp.int32, (copies, copies), 1)
    held = table == lax.broadcasted_iota(jnp.int32, (copies, copies), 0)
    first = jnp.sum(jnp.where(held & (copy < experts), copy, 0), axis=1, keepdims=True)
    second = jnp.sum(jnp.where(held & (copy >= experts), copy, 0), axis=1, keepdims=True)
    hot = second > 0
    target = jnp.where(hot & ((rank & 1) == 1), second, first)
    place = jnp.where(hot, rank >> 1, rank)
    row = ((target >> 3) * 4 + (target & 3)) * CAP + place
    row = jnp.where(((target >> 2) & 1) == half, row, -1)
    number = lax.broadcasted_iota(jnp.int32, (rows, tokens), 0)
    return [
        number == jnp.sum(jnp.where(n, row, 0), axis=0, keepdims=True) for n in named
    ]


def either(marks):
    return sum(m.astype(F32) for m in marks)


def weighted(marks, probs):
    return sum(jnp.where(m, probs[k : k + 1, :], 0.0) for k, m in enumerate(marks))


def pack_kernel(half_ref, meta_ref, table_ref, x_ref, g_ref, out_ref):
    meta = meta_ref[...]
    copies = out_ref.shape[0]
    marks = row_marks(meta, table_ref[...], half_ref[0], copies * CAP)
    onehot = either(marks).astype(BF16)
    weight = jnp.sum(weighted(marks, probabilities(meta)), axis=1, keepdims=True)
    x = dot(onehot, x_ref[...], 1, 0)
    g = dot(onehot, g_ref[...], 1, 0) * weight
    for i in range(copies):
        rows = slice(i * CAP, (i + 1) * CAP)
        out_ref[i] = jnp.concatenate([x[rows], g[rows]], axis=0).astype(BF16)


def pack(half, meta, table, x, g):
    width = x.shape[1]
    return pl.pallas_call(
        pack_kernel,
        out_shape=jax.ShapeDtypeStruct((16, 2 * CAP, width), BF16),
        in_specs=[SCALAR] + [ANYWHERE] * 4,
        out_specs=ANYWHERE,
        compiler_params=pltpu.CompilerParams(vmem_limit_bytes=VMEM_BYTES),
        cost_estimate=pl.CostEstimate(
            flops=64 * CAP * x.size, bytes_accessed=4 * x.size + 64 * CAP * width, transcendentals=0
        ),
        name="pack",
    )(half, meta, table, x, g)


def halves(ref):
    both = [ref[i].astype(F32) for i in range(ref.shape[0])]
    first = jnp.concatenate([b[:CAP] for b in both], axis=0).astype(BF16)
    second = jnp.concatenate([b[CAP:] for b in both], axis=0).astype(BF16)
    return first, second


def split_dot(weights, rows):
    high = weights.astype(BF16)
    low = (weights - high.astype(F32)).astype(BF16)
    return dot(high, rows, 0, 0) + dot(low, rows, 0, 0)


def collect_kernel(half_ref, meta_ref, table_ref, rows_ref, g_ref, *refs):
    meta = meta_ref[...]
    out_rows, back_rows = halves(rows_ref)
    marks = row_marks(meta, table_ref[...], half_ref[0], out_rows.shape[0])
    probs = probabilities(meta)
    out = split_dot(weighted(marks, probs), out_rows)
    back = dot(either(marks).astype(BF16), back_rows, 0, 0)
    products = dot(out_rows, g_ref[...], 1, 1)
    grads = jnp.concatenate(
        [jnp.sum(jnp.where(m, products, 0.0), axis=0, keepdims=True) for m in marks], axis=0
    )
    tokens = out.shape[0]
    if len(refs) > 1:
        other_ref, out_ref, back_ref, logit_ref = refs
        out_ref[...] = (out + other_ref[:tokens, :].astype(F32)).astype(BF16)
        back_ref[...] = (back + other_ref[tokens : 2 * tokens, :].astype(F32)).astype(BF16)
        three = other_ref[2 * tokens :, : grads.shape[1]].astype(F32)
        grads = grads + (three[0:4] + three[4:8] + three[8:12])
        logit_ref[...] = probs * (grads - jnp.sum(probs * grads, axis=0, keepdims=True))
    else:
        high = grads.astype(BF16).astype(F32)
        middle = (grads - high).astype(BF16).astype(F32)
        low = grads - high - middle
        three = jnp.concatenate([high, middle, low, jnp.zeros_like(low)], axis=0)
        rest = jnp.zeros((16, out.shape[1] - three.shape[1]), F32)
        refs[0][...] = jnp.concatenate(
            [out, back, jnp.concatenate([three, rest], axis=1)], axis=0
        ).astype(BF16)


def collect(half, meta, table, rows, g, *other):
    tokens, width = g.shape
    whole = jax.ShapeDtypeStruct(g.shape, BF16)
    if other:
        shapes = (whole, whole, jax.ShapeDtypeStruct((4, tokens), F32))
    else:
        shapes = jax.ShapeDtypeStruct((2 * tokens + 16, width), BF16)
    return pl.pallas_call(
        collect_kernel,
        out_shape=shapes,
        in_specs=[SCALAR] + [ANYWHERE] * (4 + len(other)),
        out_specs=(ANYWHERE,) * 3 if other else ANYWHERE,
        compiler_params=pltpu.CompilerParams(vmem_limit_bytes=VMEM_BYTES),
        cost_estimate=pl.CostEstimate(
            flops=4 * rows.size * tokens, bytes_accessed=2 * rows.size + 8 * g.size, transcendentals=0
        ),
        name="collect_last" if other else "collect",
    )(half, meta, table, rows, g, *other)


def expert_kernel(in_ref, wg_ref, wu_ref, wd_ref, out_ref, x_rows, g_rows, out_sum, back_sum):
    step = pl.program_id(0)
    copies = in_ref.shape[0]

    @pl.when(step == 0)
    def _():
        x_rows[...], g_rows[...] = halves(in_ref)

    x = x_rows[...]
    gate = dot(x, wg_ref[...], 1, 0)
    up = dot(x, wu_ref[...], 1, 0)
    hidden_grad = dot(g_rows[...], wd_ref[...], 1, 1)
    sigmoid = jax.nn.sigmoid(gate)
    hidden = (gate * sigmoid * up).astype(BF16)
    gate_grad = (hidden_grad * up * sigmoid * (1.0 + gate * (1.0 - sigmoid))).astype(BF16)
    up_grad = (hidden_grad * gate * sigmoid).astype(BF16)
    out = dot(hidden, wd_ref[...], 1, 0)
    back = dot(gate_grad, wg_ref[...], 1, 1) + dot(up_grad, wu_ref[...], 1, 1)

    @pl.when(step == 0)
    def _():
        out_sum[...] = out
        back_sum[...] = back

    @pl.when(step > 0)
    def _():
        out_sum[...] += out
        back_sum[...] += back

    @pl.when(step == pl.num_programs(0) - 1)
    def _():
        for i in range(copies):
            rows = slice(i * CAP, (i + 1) * CAP)
            out_ref[i] = jnp.concatenate([out_sum[rows, :], back_sum[rows, :]], axis=0).astype(BF16)


BLOCK = 256


def expert(both, w_gu, w_dn):
    copies, _, width = both.shape
    hidden = w_dn.shape[0]
    steps = hidden // BLOCK
    rows = copies * CAP
    return pl.pallas_call(
        expert_kernel,
        grid=(steps,),
        out_shape=jax.ShapeDtypeStruct(both.shape, BF16),
        in_specs=[
            pl.BlockSpec(both.shape, lambda j: (0, 0, 0)),
            pl.BlockSpec((width, BLOCK), lambda j: (0, j)),
            pl.BlockSpec((width, BLOCK), lambda j: (0, steps + j)),
            pl.BlockSpec((BLOCK, width), lambda j: (j, 0)),
        ],
        out_specs=pl.BlockSpec(both.shape, lambda j: (0, 0, 0)),
        scratch_shapes=[pltpu.VMEM((rows, width), BF16)] * 2 + [pltpu.VMEM((rows, width), F32)] * 2,
        compiler_params=pltpu.CompilerParams(vmem_limit_bytes=VMEM_BYTES),
        cost_estimate=pl.CostEstimate(
            flops=12 * rows * width * hidden,
            bytes_accessed=6 * width * hidden + 8 * rows * width,
            transcendentals=rows * hidden,
        ),
        name="expert",
    )(both, w_gu, w_gu, w_dn)


def after(x, *earlier):
    return lax.optimization_barrier((x, *earlier))[0]


def shifted(x, by):
    sections = SIZES[0] * SIZES[1]
    pairs = [(i, i + by) for i in range(sections) if 0 <= i + by < sections]
    here = lax.axis_index(SECTION) == (0 if by > 0 else sections - 1)
    return jnp.where(here, x, lax.ppermute(x, SECTION, pairs))


def swapped(x, cores=(0, 1)):
    pairs = [(2 * c + h, 2 * c + 1 - h) for c in cores for h in range(2)]
    return lax.ppermute(x, ("core", "z_hi"), pairs)


def exchanged(rows):
    return lax.all_to_all(rows, PLANE, split_axis=0, concat_axis=0, tiled=True)


def local(x_held, grad_held, expert_ids, gate_logits, placement, w_gate_up, w_down):
    w_gu = w_gate_up[0, 0]
    w_dn = w_down[0, 0]
    half = lax.axis_index("z_hi").astype(jnp.int32).reshape(1)
    table = placement
    odd = lax.axis_index("core") == 1

    meta = jnp.concatenate([expert_ids[0].astype(F32).T, gate_logits[0].T], axis=0)
    meta_other = swapped(meta)
    x = shifted(x_held[0], 1)
    g = shifted(grad_held[0], -1)
    x_odd = lax.ppermute(
        x_held[0],
        SECTION + ("z_hi",),
        [(4 * i + h, 4 * i + 3 - h) for i in range(SIZES[0]) for h in range(2)],
    )
    x_even = swapped(after(x, g), (0,))
    packed = after(pack(half, meta, table, x, g), x_even, x_odd)
    rows = exchanged(packed)
    g_other = swapped(after(g, packed))
    x_other = jnp.where(odd, x_odd, x_even)
    rows_other = exchanged(after(pack(half, meta_other, table, x_other, g_other), rows))

    done = expert(rows, w_gu, w_dn)
    done_other = exchanged(expert(rows_other, w_gu, w_dn))
    part = swapped(collect(half, meta_other, table, done_other, g_other))
    done = exchanged(after(done, done_other))
    section_out, input_grad, logit_grad = collect(half, meta, table, done, g, part)
    return section_out[None], input_grad[None], logit_grad.T[None]


def solution(mesh):
    fine = Mesh(mesh.devices.reshape(SIZES), SECTION + EXPERT)
    placed = (
        P(SECTION, EXPERT, None),
        P(SECTION, EXPERT, None),
        P(SECTION, EXPERT, None),
        P(SECTION, EXPERT, None),
        P(SECTION, None),
        P(SECTION, EXPERT, None, None),
        P(SECTION, EXPERT, None, None),
    )
    return jax.shard_map(
        local,
        mesh=fine,
        in_specs=placed,
        out_specs=(P(SECTION, EXPERT, None),) * 3,
        check_vma=False,
    )
```

time: 264 us -> 233 us (0.88)
  starting transfers between devices: 72.8 us -> 52.4 us
  Pallas kernels: 49.2 us -> 35.3 us
  blocking collectives: 26.4 us -> 35.5 us
  local copies, waits for them, and re-layouts: 16.6 us -> 13 us
    all_to_all x7 -> x3, starting transfers between devices: 46.5 us -> 17.7 us  [exchanged(): return lax.all_to_all(rows, PLANE, split_axis=0, concat_axis=0, tiled=True)]
    pallas_call x12 -> x6, Pallas kernels: 49.2 us -> 35.3 us  [the longest x2 27.1 us: expert(): pl.pallas_call(expert_kernel, grid=(steps,), out_shape=jax.ShapeDtypeStru...]
    all_to_all x1, blocking collectives: 26.4 us -> 35.5 us  [exchanged(): return lax.all_to_all(rows, PLANE, split_axis=0, concat_axis=0, tiled=True)]
    ppermute x8 -> x7, starting transfers between devices: 26.3 us -> 34.7 us  [the longest x4 22.2 us: swapped(): return lax.ppermute(x, ('core', 'z_hi'), pairs)]
    ppermute x8 -> x7, waiting for transfers between devices: 64.7 us -> 58.6 us  [the longest x4 58.6 us: swapped(): return lax.ppermute(x, ('core', 'z_hi'), pairs)]
    all_to_all x7 -> x3, waiting for transfers between devices: 29.5 us -> 34.1 us  [exchanged(): return lax.all_to_all(rows, PLANE, split_axis=0, concat_axis=0, tiled=True)]
    unnamed x38 -> x28, local copies, waits for them, and re-layouts: 16.6 us -> 13 us
  transfers between devices with their start and end apart: 15 -> 10, of which waited for: 10 -> 5; matrix products, arithmetic and copies ran while one was open for 1% -> 1% of each run, Pallas kernels for 17% -> 8%
where the time goes in v3:
time: 233 us; the launch traced here: 232 us
  waiting for transfers between devices  92.7 us (40%)
  starting transfers between devices  52.4 us (22%)
  blocking collectives  35.5 us (15%)
  Pallas kernels  35.3 us (15%)
  local copies, waits for them, and re-layouts  13 us (6%)
  other arithmetic  2.45 us (1%)
    ppermute x4, waiting for transfers between devices, swapped(): return lax.ppermute(x, ('core', 'z_hi'), pairs)  58.6 us
    all_to_all x1, blocking collectives, exchanged(): return lax.all_to_all(rows, PLANE, split_axis=0, concat_axis=0, tiled=True)  35.5 us
    all_to_all x3, waiting for transfers between devices, exchanged(): return lax.all_to_all(rows, PLANE, split_axis=0, concat_axis=0, tiled=True)  34.1 us
    pallas_call x2, Pallas kernels, expert(): pl.pallas_call(expert_kernel, grid=(steps,), out_shape=jax.ShapeDtypeStru...  27.1 us
    ppermute x4, starting transfers between devices, swapped(): return lax.ppermute(x, ('core', 'z_hi'), pairs)  22.2 us
    all_to_all x3, starting transfers between devices, exchanged(): return lax.all_to_all(rows, PLANE, split_axis=0, concat_axis=0, tiled=True)  17.7 us
    unnamed x28, local copies, waits for them, and re-layouts  13 us
    ppermute x1, starting transfers between devices, local(): lax.ppermute(x_held[0], SECTION + ('z_hi',), [(4 * i + h, 4 * i + 3 - h)...  8.01 us
  transfers between devices with their start and end apart: 10, of which 5 were waited for; matrix products, arithmetic and copies ran while one was open for 1% of the time, Pallas kernels for 8%

profile of v3, /device:TPU:66, one launch (start us, length us, event | category | flops | bytes accessed | tf_op | source)
XLA Modules:
  0.0 232.3 jit_solution(12192715967123320869)
XLA Ops:
  0.7 2.1 collective-permute-start.1
  2.7 2.4 %collective-permute-start = (bf16[128,2048]{1,0:T(8,128)(2,1)}, bf16[128,2048]{1,0:T(8,128)(2,1)S(1)}, u32[]{:S(2)}, u32[]{:S(2)}) collective-permute-start(bf16[128,2048]{1,0:T(8,128)(2,1)} %bitcast.20), channel_id=1, source_target_pairs={{0,32},{32,64},{64,96},{96,128},{128,160},{160,192},{192,224},{1,3... | collective-permute-start | bytes 1572872 | tf_op jit(solution)/shard_map/ppermute | solution.py:232
  5.1 8.0 %collective-permute-start.3 = (bf16[128,2048]{1,0:T(8,128)(2,1)}, bf16[128,2048]{1,0:T(8,128)(2,1)S(1)}, u32[]{:S(2)}, u32[]{:S(2)}) collective-permute-start(bf16[128,2048]{1,0:T(8,128)(2,1)} %bitcast.21), channel_id=1, source_target_pairs={{0,36},{4,32},{64,100},{68,96},{128,164},{132,160},{192,228},{196,... | collective-permute-start | bytes 1572872 | tf_op jit(solution)/shard_map/ppermute | solution.py:255
  13.2 1.1 broadcast_select_fusion.1.g_ref
  14.3 1.3 broadcast_select_fusion.2.x_ref
  15.6 12.0 %collective-permute-start.2 = (bf16[128,2048]{1,0:T(8,128)(2,1)S(1)}, bf16[128,2048]{1,0:T(8,128)(2,1)S(1)}, u32[]{:S(2)}, u32[]{:S(2)}) collective-permute-start(bf16[128,2048]{1,0:T(8,128)(2,1)S(1)} %broadcast_select_fusion.2.x_ref), channel_id=1, source_target_pairs={{0,4},{4,0},{1,5},{5,1},{2,6},{6,2},{3,7},{7,3},{8,12},{12,8},{9,1... | collective-permute-start | bytes 1572872 | tf_op jit(solution)/shard_map/ppermute | solution.py:237
  27.6 2.8 %pack.2 = bf16[16,48,2048]{2,1,0:T(8,128)(2,1)} custom-call(s32[1]{0:T(128)} %bitcast.half_ref, f32[8,128]{1,0:T(8,128)S(1)} %pad_maximum_fusion.meta_ref, s32[1,32]{1,0:T(1,128)S(1)} %copy-done.11, bf16[128,2048]{1,0:T(8,128)(2,1)S(1)} %broadcast_select_fusion.2.x_ref, bf16[128,2048]{1,0:T(8,128)(2,1)S(1)} %broadcast_select_fusion.1.g_ref), custom_call_target="tpu_custom_call" | custom-call | flops 402653184 | bytes 4194304 | tf_op jit(solution)/shard_map/pack/pallas_call | solution.py:82
  30.5 10.3 %collective-permute-done.2 = bf16[128,2048]{1,0:T(8,128)(2,1)S(1)} collective-permute-done((bf16[128,2048]{1,0:T(8,128)(2,1)S(1)}, bf16[128,2048]{1,0:T(8,128)(2,1)S(1)}, u32[]{:S(2)}, u32[]{:S(2)}) %collective-permute-start.2) | collective-permute-done | bytes 524320 | tf_op jit(solution)/shard_map/ppermute | solution.py:237
  40.7 7.5 %all-to-all-start = ((bf16[16,48,2048]{2,1,0:T(8,128)(2,1)}), bf16[16,48,2048]{2,1,0:T(8,128)(2,1)}, u32[]{:S(2)}, u32[]{:S(2)}) async-start(bf16[16,48,2048]{2,1,0:T(8,128)(2,1)} %pack.2), calls=%async_computation | async-start | bytes 6291456 | tf_op jit(solution)/shard_map/all_to_all | solution.py:241
  48.2 2.6 %collective-permute-start.5 = (bf16[128,2048]{1,0:T(8,128)(2,1)S(1)}, bf16[128,2048]{1,0:T(8,128)(2,1)S(1)}, u32[]{:S(2)}, u32[]{:S(2)}) collective-permute-start(bf16[128,2048]{1,0:T(8,128)(2,1)S(1)} %broadcast_select_fusion.1.g_ref), channel_id=1, source_target_pairs={{0,4},{4,0},{32,36},{36,32},{1,5},{5,1},{33,37},{37,33},{2,6},{6,2... | collective-permute-start | bytes 1572872 | tf_op jit(solution)/shard_map/ppermute | solution.py:237
  50.8 3.4 %collective-permute-start.4 = (f32[8,128]{1,0:T(8,128)S(1)}, f32[8,128]{1,0:T(8,128)S(1)}, u32[]{:S(2)}, u32[]{:S(2)}) collective-permute-start(f32[8,128]{1,0:T(8,128)S(1)} %pad_maximum_fusion.meta_ref), channel_id=1, source_target_pairs={{0,4},{4,0},{32,36},{36,32},{1,5},{5,1},{33,37},{37,33},{2,6},{6,2... | collective-permute-start | bytes 12296 | tf_op jit(solution)/shard_map/ppermute | solution.py:237
  54.3 11.4 %collective-permute-done.4.meta_ref = f32[8,128]{1,0:T(8,128)S(1)} collective-permute-done((f32[8,128]{1,0:T(8,128)S(1)}, f32[8,128]{1,0:T(8,128)S(1)}, u32[]{:S(2)}, u32[]{:S(2)}) %collective-permute-start.4) | collective-permute-done | bytes 4128 | tf_op jit(solution)/shard_map/ppermute | solution.py:237
  66.4 1.0 copy-done.7
  67.5 1.2 pack.3
  68.6 14.4 %all-to-all-done.in_ref = bf16[16,48,2048]{2,1,0:T(8,128)(2,1)} async-done(((bf16[16,48,2048]{2,1,0:T(8,128)(2,1)}), bf16[16,48,2048]{2,1,0:T(8,128)(2,1)}, u32[]{:S(2)}, u32[]{:S(2)}) %all-to-all-start) | async-done | bytes 3145760 | tf_op jit(solution)/shard_map/all_to_all | solution.py:241
  83.0 35.5 %all_to_all.20.in_ref = bf16[16,48,2048]{2,1,0:T(8,128)(2,1)} all-to-all(bf16[16,48,2048]{2,1,0:T(8,128)(2,1)S(1)} %pack.3), channel_id=1, replica_groups=mesh['z_lo'=4,'core'=2,'y'=4,'z_hi'=2,'x'=4] {'y','x'}, dimensions={0} | all-to-all | bytes 6291456 | tf_op jit(solution)/shard_map/all_to_all | solution.py:241
  118.5 13.5 %expert.3 = bf16[16,48,2048]{2,1,0:T(8,128)(2,1)S(1)} custom-call(bf16[16,48,2048]{2,1,0:T(8,128)(2,1)} %all_to_all.20.in_ref, bf16[2048,1536]{1,0:T(8,128)(2,1)} %bitcast.23, bf16[2048,1536]{1,0:T(8,128)(2,1)} %bitcast.24, bf16[768,2048]{1,0:T(8,128)(2,1)} %bitcast.27), custom_call_target="tpu_custom_call" | custom-call | flops 7247757312 | bytes 15728640 | tf_op jit(solution)/shard_map/expert/pallas_call | solution.py:202
  132.0 1.7 copy-done.5
  133.7 5.0 %all-to-all-start.2 = ((bf16[16,48,2048]{2,1,0:T(8,128)(2,1)}), bf16[16,48,2048]{2,1,0:T(8,128)(2,1)S(1)}, u32[]{:S(2)}, u32[]{:S(2)}) async-start(bf16[16,48,2048]{2,1,0:T(8,128)(2,1)} %copy-done.5), calls=%async_computation.2 | async-start | bytes 6291456 | tf_op jit(solution)/shard_map/all_to_all | solution.py:241
  138.7 13.5 %expert.2 = bf16[16,48,2048]{2,1,0:T(8,128)(2,1)S(1)} custom-call(bf16[16,48,2048]{2,1,0:T(8,128)(2,1)} %all-to-all-done.in_ref, bf16[2048,1536]{1,0:T(8,128)(2,1)} %bitcast.25, bf16[2048,1536]{1,0:T(8,128)(2,1)} %bitcast.26, bf16[768,2048]{1,0:T(8,128)(2,1)} %bitcast.28), custom_call_target="tpu_custom_call" | custom-call | flops 7247757312 | bytes 15728640 | tf_op jit(solution)/shard_map/expert/pallas_call | solution.py:202
  152.3 1.6 copy-done.4
  153.9 19.8 %all-to-all-done.2.rows_ref = bf16[16,48,2048]{2,1,0:T(8,128)(2,1)S(1)} async-done(((bf16[16,48,2048]{2,1,0:T(8,128)(2,1)}), bf16[16,48,2048]{2,1,0:T(8,128)(2,1)S(1)}, u32[]{:S(2)}, u32[]{:S(2)}) %all-to-all-start.2) | async-done | bytes 3145760 | tf_op jit(solution)/shard_map/all_to_all | solution.py:241
  173.7 1.7 copy-done
  175.3 5.2 %all-to-all-start.3 = ((bf16[16,48,2048]{2,1,0:T(8,128)(2,1)}), bf16[16,48,2048]{2,1,0:T(8,128)(2,1)S(1)}, u32[]{:S(2)}, u32[]{:S(2)}) async-start(bf16[16,48,2048]{2,1,0:T(8,128)(2,1)} %copy-done.4), calls=%async_computation.3 | async-start | bytes 6291456 | tf_op jit(solution)/shard_map/all_to_all | solution.py:241
  180.6 1.9 copy-done.1
  182.5 1.0 copy-done.8
  183.5 1.8 collect.1
  185.3 4.2 %collective-permute-start.6 = (bf16[272,2048]{1,0:T(8,128)(2,1)S(1)}, bf16[272,2048]{1,0:T(8,128)(2,1)S(1)}, u32[]{:S(2)}, u32[]{:S(2)}) collective-permute-start(bf16[272,2048]{1,0:T(8,128)(2,1)S(1)} %collect.1), channel_id=1, source_target_pairs={{0,4},{4,0},{32,36},{36,32},{1,5},{5,1},{33,37},{37,33},{2,6},{6,2... | collective-permute-start | bytes 3342344 | tf_op jit(solution)/shard_map/ppermute | solution.py:237
  189.5 37.0 %collective-permute-done.6.refs_0_ = bf16[272,2048]{1,0:T(8,128)(2,1)S(1)} collective-permute-done((bf16[272,2048]{1,0:T(8,128)(2,1)S(1)}, bf16[272,2048]{1,0:T(8,128)(2,1)S(1)}, u32[]{:S(2)}, u32[]{:S(2)}) %collective-permute-start.6) | collective-permute-done | bytes 1114144 | tf_op jit(solution)/shard_map/ppermute | solution.py:237
  227.5 1.0 copy-done.3
  228.5 1.2 copy-done.10
  229.8 2.5 %collect_last.1 = (bf16[128,2048]{1,0:T(8,128)(2,1)}, bf16[128,2048]{1,0:T(8,128)(2,1)}, f32[4,128]{1,0:T(4,128)}) custom-call(s32[1]{0:T(128)} %bitcast.half_ref, f32[8,128]{1,0:T(8,128)S(1)} %pad_maximum_fusion.meta_ref, s32[1,32]{1,0:T(1,128)S(1)} %copy-done.11, bf16[16,48,2048]{2,1,0:T(8,128)(2,1)S(1)} %all-to-all-done.3.rows_ref, ...), custom_call_target="tpu_custom_call" | custom-call | flops 805306368 | bytes 5242880 | tf_op jit(solution)/shard_map/collect_last/pallas_call | solution.py:145
  (28 shorter events, 1.9 us)
Async XLA Ops:
  0.6 27.0 %copy-start.12 = (s32[1,128,4]{1,2,0:T(4,128)S(1)}, s32[1,128,4]{1,2,0:T(4,128)}, u32[]{:S(2)}) copy-start(s32[1,128,4]{1,2,0:T(4,128)} %param.9) | copy-start | bytes 6148
  0.6 27.0 %copy-start.13 = (f32[1,128,4]{1,2,0:T(4,128)S(1)}, f32[1,128,4]{1,2,0:T(4,128)}, u32[]{:S(2)}) copy-start(f32[1,128,4]{1,2,0:T(4,128)} %param.10) | copy-start | bytes 6148
  0.7 27.0 %copy-start.11 = (s32[1,32]{1,0:T(1,128)S(1)}, s32[1,32]{1,0:T(1,128)}, u32[]{:S(2)}) copy-start(s32[1,32]{1,0:T(1,128)} %table_ref.7) | copy-start | bytes 388
  0.7 12.5 %collective-permute-start.1 = (bf16[128,2048]{1,0:T(8,128)(2,1)}, bf16[128,2048]{1,0:T(8,128)(2,1)S(1)}, u32[]{:S(2)}, u32[]{:S(2)}) collective-permute-start(bf16[128,2048]{1,0:T(8,128)(2,1)} %bitcast.19), channel_id=1, source_target_pairs={{32,0},{64,32},{96,64},{128,96},{160,128},{192,160},{224,192},{33,... | collective-permute-start | bytes 1572872 | tf_op jit(solution)/shard_map/ppermute | solution.py:232
  2.7 11.6 %collective-permute-start = (bf16[128,2048]{1,0:T(8,128)(2,1)}, bf16[128,2048]{1,0:T(8,128)(2,1)S(1)}, u32[]{:S(2)}, u32[]{:S(2)}) collective-permute-start(bf16[128,2048]{1,0:T(8,128)(2,1)} %bitcast.20), channel_id=1, source_target_pairs={{0,32},{32,64},{64,96},{96,128},{128,160},{160,192},{192,224},{1,3... | collective-permute-start | bytes 1572872 | tf_op jit(solution)/shard_map/ppermute | solution.py:232
  5.1 25.3 %collective-permute-start.3 = (bf16[128,2048]{1,0:T(8,128)(2,1)}, bf16[128,2048]{1,0:T(8,128)(2,1)S(1)}, u32[]{:S(2)}, u32[]{:S(2)}) collective-permute-start(bf16[128,2048]{1,0:T(8,128)(2,1)} %bitcast.21), channel_id=1, source_target_pairs={{0,36},{4,32},{64,100},{68,96},{128,164},{132,160},{192,228},{196,... | collective-permute-start | bytes 1572872 | tf_op jit(solution)/shard_map/ppermute | solution.py:255
  14.3 33.9 %copy-start.2 = (bf16[128,2048]{1,0:T(8,128)(2,1)}, bf16[128,2048]{1,0:T(8,128)(2,1)S(1)}, u32[]{:S(2)}) copy-start(bf16[128,2048]{1,0:T(8,128)(2,1)S(1)} %broadcast_select_fusion.1.g_ref) | copy-start | bytes 1572868
  15.6 25.1 %collective-permute-start.2 = (bf16[128,2048]{1,0:T(8,128)(2,1)S(1)}, bf16[128,2048]{1,0:T(8,128)(2,1)S(1)}, u32[]{:S(2)}, u32[]{:S(2)}) collective-permute-start(bf16[128,2048]{1,0:T(8,128)(2,1)S(1)} %broadcast_select_fusion.2.x_ref), channel_id=1, source_target_pairs={{0,4},{4,0},{1,5},{5,1},{2,6},{6,2},{3,7},{7,3},{8,12},{12,8},{9,1... | collective-permute-start | bytes 1572872 | tf_op jit(solution)/shard_map/ppermute | solution.py:237
  40.7 42.3 %all-to-all-start = ((bf16[16,48,2048]{2,1,0:T(8,128)(2,1)}), bf16[16,48,2048]{2,1,0:T(8,128)(2,1)}, u32[]{:S(2)}, u32[]{:S(2)}) async-start(bf16[16,48,2048]{2,1,0:T(8,128)(2,1)} %pack.2), calls=%async_computation | async-start | bytes 6291456 | tf_op jit(solution)/shard_map/all_to_all | solution.py:241
  48.2 17.4 %collective-permute-start.5 = (bf16[128,2048]{1,0:T(8,128)(2,1)S(1)}, bf16[128,2048]{1,0:T(8,128)(2,1)S(1)}, u32[]{:S(2)}, u32[]{:S(2)}) collective-permute-start(bf16[128,2048]{1,0:T(8,128)(2,1)S(1)} %broadcast_select_fusion.1.g_ref), channel_id=1, source_target_pairs={{0,4},{4,0},{32,36},{36,32},{1,5},{5,1},{33,37},{37,33},{2,6},{6,2... | collective-permute-start | bytes 1572872 | tf_op jit(solution)/shard_map/ppermute | solution.py:237
  50.8 14.8 %collective-permute-start.4 = (f32[8,128]{1,0:T(8,128)S(1)}, f32[8,128]{1,0:T(8,128)S(1)}, u32[]{:S(2)}, u32[]{:S(2)}) collective-permute-start(f32[8,128]{1,0:T(8,128)S(1)} %pad_maximum_fusion.meta_ref), channel_id=1, source_target_pairs={{0,4},{4,0},{32,36},{36,32},{1,5},{5,1},{33,37},{37,33},{2,6},{6,2... | collective-permute-start | bytes 12296 | tf_op jit(solution)/shard_map/ppermute | solution.py:237
  65.6 0.8 copy-start.6
  66.4 1.0 copy-start.7
  132.0 1.7 copy-start.5
  133.7 40.0 %all-to-all-start.2 = ((bf16[16,48,2048]{2,1,0:T(8,128)(2,1)}), bf16[16,48,2048]{2,1,0:T(8,128)(2,1)S(1)}, u32[]{:S(2)}, u32[]{:S(2)}) async-start(bf16[16,48,2048]{2,1,0:T(8,128)(2,1)} %copy-done.5), calls=%async_computation.2 | async-start | bytes 6291456 | tf_op jit(solution)/shard_map/all_to_all | solution.py:241
  152.2 1.6 copy-start.4
  173.7 1.7 copy-start
  175.3 52.1 %all-to-all-start.3 = ((bf16[16,48,2048]{2,1,0:T(8,128)(2,1)}), bf16[16,48,2048]{2,1,0:T(8,128)(2,1)S(1)}, u32[]{:S(2)}, u32[]{:S(2)}) async-start(bf16[16,48,2048]{2,1,0:T(8,128)(2,1)} %copy-done.4), calls=%async_computation.3 | async-start | bytes 6291456 | tf_op jit(solution)/shard_map/all_to_all | solution.py:241
  180.6 1.9 copy-start.1
  182.5 1.0 copy-start.8
  185.3 41.2 %collective-permute-start.6 = (bf16[272,2048]{1,0:T(8,128)(2,1)S(1)}, bf16[272,2048]{1,0:T(8,128)(2,1)S(1)}, u32[]{:S(2)}, u32[]{:S(2)}) collective-permute-start(bf16[272,2048]{1,0:T(8,128)(2,1)S(1)} %collect.1), channel_id=1, source_target_pairs={{0,4},{4,0},{32,36},{36,32},{1,5},{5,1},{33,37},{37,33},{2,6},{6,2... | collective-permute-start | bytes 3342344 | tf_op jit(solution)/shard_map/ppermute | solution.py:237
  226.5 1.0 copy-start.9
  227.5 1.0 copy-start.3
  228.5 1.2 copy-start.10

commit v4 on v3

--- a/solution.py
+++ b/solution.py
@@ -14,7 +14,8 @@
 PLANE = ("y", "x")
 SIZES = (4, 2, 4, 2, 4)
 CAP = 24
-VMEM_BYTES = 48 * 1024 * 1024
+VMEM_BYTES = 28 * 1024 * 1024
+EXPERT_BYTES = 40 * 1024 * 1024
 ANYWHERE = pl.BlockSpec(memory_space=pltpu.VMEM)
 SCALAR = pl.BlockSpec(memory_space=pltpu.SMEM)
 
@@ -211,7 +212,7 @@
         ],
         out_specs=pl.BlockSpec(both.shape, lambda j: (0, 0, 0)),
         scratch_shapes=[pltpu.VMEM((rows, width), BF16)] * 2 + [pltpu.VMEM((rows, width), F32)] * 2,
-        compiler_params=pltpu.CompilerParams(vmem_limit_bytes=VMEM_BYTES),
+        compiler_params=pltpu.CompilerParams(vmem_limit_bytes=EXPERT_BYTES),
         cost_estimate=pl.CostEstimate(
             flops=12 * rows * width * hidden,
             bytes_accessed=6 * width * hidden + 8 * rows * width,
@@ -257,7 +258,7 @@
         SECTION + ("z_hi",),
         [(4 * i + h, 4 * i + 3 - h) for i in range(SIZES[0]) for h in range(2)],
     )
-    x_even = swapped(after(x, g), (0,))
+    x_even = swapped(after(x, g, x_odd), (0,))
     packed = after(pack(half, meta, table, x, g), x_even, x_odd)
     rows = exchanged(packed)
     g_other = swapped(after(g, packed))

time: 233 us -> 231 us (level)
  waiting for transfers between devices: 92.7 us -> 97.5 us
  starting transfers between devices: 52.4 us -> 48.1 us
  Pallas kernels: 35.3 us -> 32.9 us
  blocking collectives: 35.5 us -> 33.1 us
    ppermute x1, waiting for transfers between devices: 0.01 us -> 10.1 us  [local(): lax.ppermute(x_held[0], SECTION + ('z_hi',), [(4 * i + h, 4 * i + 3 - h)...]
    ppermute x4, starting transfers between devices: 22.2 us -> 13.7 us  [swapped(): return lax.ppermute(x, ('core', 'z_hi'), pairs)]
    all_to_all x3, starting transfers between devices: 17.7 us -> 22 us  [exchanged(): return lax.all_to_all(rows, PLANE, split_axis=0, concat_axis=0, tiled=True)]
    all_to_all x3, waiting for transfers between devices: 34.1 us -> 30.1 us  [exchanged(): return lax.all_to_all(rows, PLANE, split_axis=0, concat_axis=0, tiled=True)]
    all_to_all x1, blocking collectives: 35.5 us -> 33.1 us  [exchanged(): return lax.all_to_all(rows, PLANE, split_axis=0, concat_axis=0, tiled=True)]
    pallas_call x2, Pallas kernels: 27.1 us -> 24.7 us  [expert(): pl.pallas_call(expert_kernel, grid=(steps,), out_shape=jax.ShapeDtypeStru...]
    unnamed x28 -> x32, local copies, waits for them, and re-layouts: 13 us -> 14.9 us
  transfers between devices with their start and end apart: 10 -> 10, of which waited for: 5 -> 6; matrix products, arithmetic and copies ran while one was open for 1% -> 1% of each run, Pallas kernels for 8% -> 8%
where the time goes in v4:
time: 231 us; the launch traced here: 230 us
  waiting for transfers between devices  97.5 us (42%)
  starting transfers between devices  48.1 us (21%)
  blocking collectives  33.1 us (14%)
  Pallas kernels  32.9 us (14%)
  local copies, waits for them, and re-layouts  14.9 us (6%)
  other arithmetic  2.45 us (1%)
    ppermute x4, waiting for transfers between devices, swapped(): return lax.ppermute(x, ('core', 'z_hi'), pairs)  57.3 us
    all_to_all x1, blocking collectives, exchanged(): return lax.all_to_all(rows, PLANE, split_axis=0, concat_axis=0, tiled=True)  33.1 us
    all_to_all x3, waiting for transfers between devices, exchanged(): return lax.all_to_all(rows, PLANE, split_axis=0, concat_axis=0, tiled=True)  30.1 us
    pallas_call x2, Pallas kernels, expert(): pl.pallas_call(expert_kernel, grid=(steps,), out_shape=jax.ShapeDtypeStru...  24.7 us
    all_to_all x3, starting transfers between devices, exchanged(): return lax.all_to_all(rows, PLANE, split_axis=0, concat_axis=0, tiled=True)  22 us
    unnamed x32, local copies, waits for them, and re-layouts  14.9 us
    ppermute x4, starting transfers between devices, swapped(): return lax.ppermute(x, ('core', 'z_hi'), pairs)  13.7 us
    ppermute x1, waiting for transfers between devices, local(): lax.ppermute(x_held[0], SECTION + ('z_hi',), [(4 * i + h, 4 * i + 3 - h)...  10.1 us
  transfers between devices with their start and end apart: 10, of which 6 were waited for; matrix products, arithmetic and copies ran while one was open for 1% of the time, Pallas kernels for 8%

profile of v4, /device:TPU:66, one launch (start us, length us, event | category | flops | bytes accessed | tf_op | source)
XLA Modules:
  0.0 229.8 jit_solution(13535325991282029468)
XLA Ops:
  0.7 2.1 collective-permute-start.1
  2.7 2.4 %collective-permute-start = (bf16[128,2048]{1,0:T(8,128)(2,1)}, bf16[128,2048]{1,0:T(8,128)(2,1)S(1)}, u32[]{:S(2)}, u32[]{:S(2)}) collective-permute-start(bf16[128,2048]{1,0:T(8,128)(2,1)} %bitcast.22), channel_id=1, source_target_pairs={{0,32},{32,64},{64,96},{96,128},{128,160},{160,192},{192,224},{1,3... | collective-permute-start | bytes 1572872 | tf_op jit(solution)/shard_map/ppermute | solution.py:233
  5.1 8.0 %collective-permute-start.2 = (bf16[128,2048]{1,0:T(8,128)(2,1)}, bf16[128,2048]{1,0:T(8,128)(2,1)S(1)}, u32[]{:S(2)}, u32[]{:S(2)}) collective-permute-start(bf16[128,2048]{1,0:T(8,128)(2,1)} %bitcast.23), channel_id=1, source_target_pairs={{0,36},{4,32},{64,100},{68,96},{128,164},{132,160},{192,228},{196,... | collective-permute-start | bytes 1572872 | tf_op jit(solution)/shard_map/ppermute | solution.py:256
  13.2 1.1 broadcast_select_fusion.1.g_ref
  14.3 1.3 broadcast_select_fusion.2.x_ref
  15.6 10.1 %collective-permute-done.2 = bf16[128,2048]{1,0:T(8,128)(2,1)S(1)} collective-permute-done((bf16[128,2048]{1,0:T(8,128)(2,1)}, bf16[128,2048]{1,0:T(8,128)(2,1)S(1)}, u32[]{:S(2)}, u32[]{:S(2)}) %collective-permute-start.2) | collective-permute-done | bytes 524320 | tf_op jit(solution)/shard_map/ppermute | solution.py:256
  25.7 5.3 %collective-permute-start.3 = (bf16[128,2048]{1,0:T(8,128)(2,1)S(1)}, bf16[128,2048]{1,0:T(8,128)(2,1)S(1)}, u32[]{:S(2)}, u32[]{:S(2)}) collective-permute-start(bf16[128,2048]{1,0:T(8,128)(2,1)S(1)} %broadcast_select_fusion.2.x_ref), channel_id=1, source_target_pairs={{0,4},{4,0},{1,5},{5,1},{2,6},{6,2},{3,7},{7,3},{8,12},{12,8},{9,1... | collective-permute-start | bytes 1572872 | tf_op jit(solution)/shard_map/ppermute | solution.py:238
  31.1 2.8 %pack.2 = bf16[16,48,2048]{2,1,0:T(8,128)(2,1)} custom-call(s32[1]{0:T(128)} %bitcast.half_ref, f32[8,128]{1,0:T(8,128)S(1)} %pad_maximum_fusion.meta_ref, s32[1,32]{1,0:T(1,128)S(1)} %copy-done.11, bf16[128,2048]{1,0:T(8,128)(2,1)S(1)} %broadcast_select_fusion.2.x_ref, bf16[128,2048]{1,0:T(8,128)(2,1)S(1)} %broadcast_select_fusion.1.g_ref), custom_call_target="tpu_custom_call" | custom-call | flops 402653184 | bytes 4194304 | tf_op jit(solution)/shard_map/pack/pallas_call | solution.py:83
  33.9 10.1 %collective-permute-done.3 = bf16[128,2048]{1,0:T(8,128)(2,1)S(1)} collective-permute-done((bf16[128,2048]{1,0:T(8,128)(2,1)S(1)}, bf16[128,2048]{1,0:T(8,128)(2,1)S(1)}, u32[]{:S(2)}, u32[]{:S(2)}) %collective-permute-start.3) | collective-permute-done | bytes 524320 | tf_op jit(solution)/shard_map/ppermute | solution.py:238
  44.1 7.5 %all-to-all-start = ((bf16[16,48,2048]{2,1,0:T(8,128)(2,1)}), bf16[16,48,2048]{2,1,0:T(8,128)(2,1)}, u32[]{:S(2)}, u32[]{:S(2)}) async-start(bf16[16,48,2048]{2,1,0:T(8,128)(2,1)} %pack.2), calls=%async_computation | async-start | bytes 6291456 | tf_op jit(solution)/shard_map/all_to_all | solution.py:242
  51.6 3.9 %collective-permute-start.5 = (bf16[128,2048]{1,0:T(8,128)(2,1)S(1)}, bf16[128,2048]{1,0:T(8,128)(2,1)S(1)}, u32[]{:S(2)}, u32[]{:S(2)}) collective-permute-start(bf16[128,2048]{1,0:T(8,128)(2,1)S(1)} %broadcast_select_fusion.1.g_ref), channel_id=1, source_target_pairs={{0,4},{4,0},{32,36},{36,32},{1,5},{5,1},{33,37},{37,33},{2,6},{6,2... | collective-permute-start | bytes 1572872 | tf_op jit(solution)/shard_map/ppermute | solution.py:238
  55.5 2.1 collective-permute-start.4
  57.6 11.3 %collective-permute-done.4.meta_ref = f32[8,128]{1,0:T(8,128)S(1)} collective-permute-done((f32[8,128]{1,0:T(8,128)S(1)}, f32[8,128]{1,0:T(8,128)S(1)}, u32[]{:S(2)}, u32[]{:S(2)}) %collective-permute-start.4) | collective-permute-done | bytes 4128 | tf_op jit(solution)/shard_map/ppermute | solution.py:238
  70.8 1.2 pack.3
  72.0 13.7 %all-to-all-done.in_ref = bf16[16,48,2048]{2,1,0:T(8,128)(2,1)} async-done(((bf16[16,48,2048]{2,1,0:T(8,128)(2,1)}), bf16[16,48,2048]{2,1,0:T(8,128)(2,1)}, u32[]{:S(2)}, u32[]{:S(2)}) %all-to-all-start) | async-done | bytes 3145760 | tf_op jit(solution)/shard_map/all_to_all | solution.py:242
  85.7 33.1 %all_to_all.20.in_ref = bf16[16,48,2048]{2,1,0:T(8,128)(2,1)S(1)} all-to-all(bf16[16,48,2048]{2,1,0:T(8,128)(2,1)S(1)} %pack.3), channel_id=1, replica_groups=mesh['z_lo'=4,'core'=2,'y'=4,'z_hi'=2,'x'=4] {'y','x'}, dimensions={0} | all-to-all | bytes 6291456 | tf_op jit(solution)/shard_map/all_to_all | solution.py:242
  118.7 11.8 %expert.3 = bf16[16,48,2048]{2,1,0:T(8,128)(2,1)S(1)} custom-call(bf16[16,48,2048]{2,1,0:T(8,128)(2,1)S(1)} %all_to_all.20.in_ref, bf16[2048,1536]{1,0:T(8,128)(2,1)} %bitcast.25, bf16[2048,1536]{1,0:T(8,128)(2,1)} %bitcast.26, bf16[768,2048]{1,0:T(8,128)(2,1)S(1)} %bitcast.19), custom_call_target="tpu_custom_call" | custom-call | flops 7247757312 | bytes 15728640 | tf_op jit(solution)/shard_map/expert/pallas_call | solution.py:203
  130.6 1.7 copy-done.5
  132.3 6.5 %all-to-all-start.2 = ((bf16[16,48,2048]{2,1,0:T(8,128)(2,1)}), bf16[16,48,2048]{2,1,0:T(8,128)(2,1)S(1)}, u32[]{:S(2)}, u32[]{:S(2)}) async-start(bf16[16,48,2048]{2,1,0:T(8,128)(2,1)} %copy-done.5), calls=%async_computation.2 | async-start | bytes 6291456 | tf_op jit(solution)/shard_map/all_to_all | solution.py:242
  138.8 1.9 copy-done.13
  140.7 12.8 %expert.2 = bf16[16,48,2048]{2,1,0:T(8,128)(2,1)S(1)} custom-call(bf16[16,48,2048]{2,1,0:T(8,128)(2,1)} %all-to-all-done.in_ref, bf16[2048,1536]{1,0:T(8,128)(2,1)} %bitcast.27, bf16[2048,1536]{1,0:T(8,128)(2,1)} %bitcast.28, bf16[768,2048]{1,0:T(8,128)(2,1)S(1)} %bitcast.20), custom_call_target="tpu_custom_call" | custom-call | flops 7247757312 | bytes 15728640 | tf_op jit(solution)/shard_map/expert/pallas_call | solution.py:203
  153.6 1.6 copy-done.4
  155.2 16.4 %all-to-all-done.2.rows_ref = bf16[16,48,2048]{2,1,0:T(8,128)(2,1)S(1)} async-done(((bf16[16,48,2048]{2,1,0:T(8,128)(2,1)}), bf16[16,48,2048]{2,1,0:T(8,128)(2,1)S(1)}, u32[]{:S(2)}, u32[]{:S(2)}) %all-to-all-start.2) | async-done | bytes 3145760 | tf_op jit(solution)/shard_map/all_to_all | solution.py:242
  171.5 1.7 copy-done
  173.2 7.9 %all-to-all-start.3 = ((bf16[16,48,2048]{2,1,0:T(8,128)(2,1)}), bf16[16,48,2048]{2,1,0:T(8,128)(2,1)S(1)}, u32[]{:S(2)}, u32[]{:S(2)}) async-start(bf16[16,48,2048]{2,1,0:T(8,128)(2,1)} %copy-done.4), calls=%async_computation.3 | async-start | bytes 6291456 | tf_op jit(solution)/shard_map/all_to_all | solution.py:242
  181.2 1.9 copy-done.1
  184.1 1.8 collect.1
  185.8 2.4 %collective-permute-start.6 = (bf16[272,2048]{1,0:T(8,128)(2,1)S(1)}, bf16[272,2048]{1,0:T(8,128)(2,1)S(1)}, u32[]{:S(2)}, u32[]{:S(2)}) collective-permute-start(bf16[272,2048]{1,0:T(8,128)(2,1)S(1)} %collect.1), channel_id=1, source_target_pairs={{0,4},{4,0},{32,36},{36,32},{1,5},{5,1},{33,37},{37,33},{2,6},{6,2... | collective-permute-start | bytes 3342344 | tf_op jit(solution)/shard_map/ppermute | solution.py:238
  188.2 35.8 %collective-permute-done.6.refs_0_ = bf16[272,2048]{1,0:T(8,128)(2,1)S(1)} collective-permute-done((bf16[272,2048]{1,0:T(8,128)(2,1)S(1)}, bf16[272,2048]{1,0:T(8,128)(2,1)S(1)}, u32[]{:S(2)}, u32[]{:S(2)}) %collective-permute-start.6) | collective-permute-done | bytes 1114144 | tf_op jit(solution)/shard_map/ppermute | solution.py:238
  225.0 1.0 copy-done.3
  226.1 1.2 copy-done.10
  227.3 2.5 %collect_last.1 = (bf16[128,2048]{1,0:T(8,128)(2,1)}, bf16[128,2048]{1,0:T(8,128)(2,1)}, f32[4,128]{1,0:T(4,128)}) custom-call(s32[1]{0:T(128)} %bitcast.half_ref, f32[8,128]{1,0:T(8,128)S(1)} %pad_maximum_fusion.meta_ref, s32[1,32]{1,0:T(1,128)S(1)} %copy-done.11, bf16[16,48,2048]{2,1,0:T(8,128)(2,1)S(1)} %all-to-all-done.3.rows_ref, ...), custom_call_target="tpu_custom_call" | custom-call | flops 805306368 | bytes 5242880 | tf_op jit(solution)/shard_map/collect_last/pallas_call | solution.py:146
  (32 shorter events, 4.0 us)
Async XLA Ops:
  0.6 30.4 %copy-start.14 = (s32[1,128,4]{1,2,0:T(4,128)S(1)}, s32[1,128,4]{1,2,0:T(4,128)}, u32[]{:S(2)}) copy-start(s32[1,128,4]{1,2,0:T(4,128)} %param.9) | copy-start | bytes 6148
  0.6 30.4 %copy-start.15 = (f32[1,128,4]{1,2,0:T(4,128)S(1)}, f32[1,128,4]{1,2,0:T(4,128)}, u32[]{:S(2)}) copy-start(f32[1,128,4]{1,2,0:T(4,128)} %param.10) | copy-start | bytes 6148
  0.7 30.4 %copy-start.11 = (s32[1,32]{1,0:T(1,128)S(1)}, s32[1,32]{1,0:T(1,128)}, u32[]{:S(2)}) copy-start(s32[1,32]{1,0:T(1,128)} %table_ref.7) | copy-start | bytes 388
  0.7 12.5 %collective-permute-start.1 = (bf16[128,2048]{1,0:T(8,128)(2,1)}, bf16[128,2048]{1,0:T(8,128)(2,1)S(1)}, u32[]{:S(2)}, u32[]{:S(2)}) collective-permute-start(bf16[128,2048]{1,0:T(8,128)(2,1)} %bitcast.21), channel_id=1, source_target_pairs={{32,0},{64,32},{96,64},{128,96},{160,128},{192,160},{224,192},{33,... | collective-permute-start | bytes 1572872 | tf_op jit(solution)/shard_map/ppermute | solution.py:233
  2.7 11.6 %collective-permute-start = (bf16[128,2048]{1,0:T(8,128)(2,1)}, bf16[128,2048]{1,0:T(8,128)(2,1)S(1)}, u32[]{:S(2)}, u32[]{:S(2)}) collective-permute-start(bf16[128,2048]{1,0:T(8,128)(2,1)} %bitcast.22), channel_id=1, source_target_pairs={{0,32},{32,64},{64,96},{96,128},{128,160},{160,192},{192,224},{1,3... | collective-permute-start | bytes 1572872 | tf_op jit(solution)/shard_map/ppermute | solution.py:233
  5.1 20.6 %collective-permute-start.2 = (bf16[128,2048]{1,0:T(8,128)(2,1)}, bf16[128,2048]{1,0:T(8,128)(2,1)S(1)}, u32[]{:S(2)}, u32[]{:S(2)}) collective-permute-start(bf16[128,2048]{1,0:T(8,128)(2,1)} %bitcast.23), channel_id=1, source_target_pairs={{0,36},{4,32},{64,100},{68,96},{128,164},{132,160},{192,228},{196,... | collective-permute-start | bytes 1572872 | tf_op jit(solution)/shard_map/ppermute | solution.py:256
  14.3 37.3 %copy-start.2 = (bf16[128,2048]{1,0:T(8,128)(2,1)}, bf16[128,2048]{1,0:T(8,128)(2,1)S(1)}, u32[]{:S(2)}) copy-start(bf16[128,2048]{1,0:T(8,128)(2,1)S(1)} %broadcast_select_fusion.1.g_ref) | copy-start | bytes 1572868
  25.7 18.3 %collective-permute-start.3 = (bf16[128,2048]{1,0:T(8,128)(2,1)S(1)}, bf16[128,2048]{1,0:T(8,128)(2,1)S(1)}, u32[]{:S(2)}, u32[]{:S(2)}) collective-permute-start(bf16[128,2048]{1,0:T(8,128)(2,1)S(1)} %broadcast_select_fusion.2.x_ref), channel_id=1, source_target_pairs={{0,4},{4,0},{1,5},{5,1},{2,6},{6,2},{3,7},{7,3},{8,12},{12,8},{9,1... | collective-permute-start | bytes 1572872 | tf_op jit(solution)/shard_map/ppermute | solution.py:238
  44.1 41.6 %all-to-all-start = ((bf16[16,48,2048]{2,1,0:T(8,128)(2,1)}), bf16[16,48,2048]{2,1,0:T(8,128)(2,1)}, u32[]{:S(2)}, u32[]{:S(2)}) async-start(bf16[16,48,2048]{2,1,0:T(8,128)(2,1)} %pack.2), calls=%async_computation | async-start | bytes 6291456 | tf_op jit(solution)/shard_map/all_to_all | solution.py:242
  51.6 17.4 %collective-permute-start.5 = (bf16[128,2048]{1,0:T(8,128)(2,1)S(1)}, bf16[128,2048]{1,0:T(8,128)(2,1)S(1)}, u32[]{:S(2)}, u32[]{:S(2)}) collective-permute-start(bf16[128,2048]{1,0:T(8,128)(2,1)S(1)} %broadcast_select_fusion.1.g_ref), channel_id=1, source_target_pairs={{0,4},{4,0},{32,36},{36,32},{1,5},{5,1},{33,37},{37,33},{2,6},{6,2... | collective-permute-start | bytes 1572872 | tf_op jit(solution)/shard_map/ppermute | solution.py:238
  55.5 13.5 %collective-permute-start.4 = (f32[8,128]{1,0:T(8,128)S(1)}, f32[8,128]{1,0:T(8,128)S(1)}, u32[]{:S(2)}, u32[]{:S(2)}) collective-permute-start(f32[8,128]{1,0:T(8,128)S(1)} %pad_maximum_fusion.meta_ref), channel_id=1, source_target_pairs={{0,4},{4,0},{32,36},{36,32},{1,5},{5,1},{33,37},{37,33},{2,6},{6,2... | collective-permute-start | bytes 12296 | tf_op jit(solution)/shard_map/ppermute | solution.py:238
  69.0 0.8 copy-start.6
  69.8 1.0 copy-start.7
  85.7 33.1 %copy-start.12 = (bf16[1,1,768,2048]{3,2,1,0:T(8,128)(2,1)S(1)}, bf16[1,1,768,2048]{3,2,1,0:T(8,128)(2,1)}, u32[]{:S(2)}) copy-start(bf16[1,1,768,2048]{3,2,1,0:T(8,128)(2,1)} %param.13) | copy-start | bytes 9437188
  130.6 1.7 copy-start.5
  132.3 39.3 %all-to-all-start.2 = ((bf16[16,48,2048]{2,1,0:T(8,128)(2,1)}), bf16[16,48,2048]{2,1,0:T(8,128)(2,1)S(1)}, u32[]{:S(2)}, u32[]{:S(2)}) async-start(bf16[16,48,2048]{2,1,0:T(8,128)(2,1)} %copy-done.5), calls=%async_computation.2 | async-start | bytes 6291456 | tf_op jit(solution)/shard_map/all_to_all | solution.py:242
  138.8 1.9 copy-start.13
  153.5 1.6 copy-start.4
  171.5 1.7 copy-start
  173.2 51.8 %all-to-all-start.3 = ((bf16[16,48,2048]{2,1,0:T(8,128)(2,1)}), bf16[16,48,2048]{2,1,0:T(8,128)(2,1)S(1)}, u32[]{:S(2)}, u32[]{:S(2)}) async-start(bf16[16,48,2048]{2,1,0:T(8,128)(2,1)} %copy-done.4), calls=%async_computation.3 | async-start | bytes 6291456 | tf_op jit(solution)/shard_map/all_to_all | solution.py:242
  181.2 1.9 copy-start.1
  183.1 1.0 copy-start.8
  185.8 38.2 %collective-permute-start.6 = (bf16[272,2048]{1,0:T(8,128)(2,1)S(1)}, bf16[272,2048]{1,0:T(8,128)(2,1)S(1)}, u32[]{:S(2)}, u32[]{:S(2)}) collective-permute-start(bf16[272,2048]{1,0:T(8,128)(2,1)S(1)} %collect.1), channel_id=1, source_target_pairs={{0,4},{4,0},{32,36},{36,32},{1,5},{5,1},{33,37},{37,33},{2,6},{6,2... | collective-permute-start | bytes 3342344 | tf_op jit(solution)/shard_map/ppermute | solution.py:238
  224.0 1.0 copy-start.9
  225.0 1.0 copy-start.3
  226.1 1.2 copy-start.10

commit v5 on v4

--- a/solution.py
+++ b/solution.py
@@ -169,9 +169,10 @@
     up = dot(x, wu_ref[...], 1, 0)
     hidden_grad = dot(g_rows[...], wd_ref[...], 1, 1)
     sigmoid = jax.nn.sigmoid(gate)
-    hidden = (gate * sigmoid * up).astype(BF16)
-    gate_grad = (hidden_grad * up * sigmoid * (1.0 + gate * (1.0 - sigmoid))).astype(BF16)
-    up_grad = (hidden_grad * gate * sigmoid).astype(BF16)
+    silu = gate * sigmoid
+    hidden = (silu * up).astype(BF16)
+    gate_grad = (hidden_grad * up * (sigmoid + silu * (1.0 - sigmoid))).astype(BF16)
+    up_grad = (hidden_grad * silu).astype(BF16)
     out = dot(hidden, wd_ref[...], 1, 0)
     back = dot(gate_grad, wg_ref[...], 1, 1) + dot(up_grad, wu_ref[...], 1, 1)
 

time: 231 us -> 230 us (level)
  no operation moved by 1% of the time
where the time goes in v5:
time: 230 us
  waiting for transfers between devices  97.6 us (42%)
  starting transfers between devices  48.1 us (21%)
  blocking collectives  33.1 us (14%)
  Pallas kernels  32.7 us (14%)
  local copies, waits for them, and re-layouts  14.9 us (6%)
  other arithmetic  2.45 us (1%)
    ppermute x4, waiting for transfers between devices, swapped(): return lax.ppermute(x, ('core', 'z_hi'), pairs)  57.3 us
    all_to_all x1, blocking collectives, exchanged(): return lax.all_to_all(rows, PLANE, split_axis=0, concat_axis=0, tiled=True)  33.1 us
    all_to_all x3, waiting for transfers between devices, exchanged(): return lax.all_to_all(rows, PLANE, split_axis=0, concat_axis=0, tiled=True)  30.2 us
    pallas_call x2, Pallas kernels, expert(): pl.pallas_call(expert_kernel, grid=(steps,), out_shape=jax.ShapeDtypeStru...  24.5 us
    all_to_all x3, starting transfers between devices, exchanged(): return lax.all_to_all(rows, PLANE, split_axis=0, concat_axis=0, tiled=True)  22 us
    unnamed x32, local copies, waits for them, and re-layouts  14.9 us
    ppermute x4, starting transfers between devices, swapped(): return lax.ppermute(x, ('core', 'z_hi'), pairs)  13.7 us
    ppermute x1, waiting for transfers between devices, local(): lax.ppermute(x_held[0], SECTION + ('z_hi',), [(4 * i + h, 4 * i + 3 - h)...  10.1 us
  transfers between devices with their start and end apart: 10, of which 6 were waited for; matrix products, arithmetic and copies ran while one was open for 1% of the time, Pallas kernels for 8%

profile of v5, /device:TPU:66, one launch (start us, length us, event | category | flops | bytes accessed | tf_op | source)
XLA Modules:
  0.0 229.7 jit_solution(5684392633383941159)
XLA Ops:
  0.7 2.1 collective-permute-start.1
  2.7 2.4 %collective-permute-start = (bf16[128,2048]{1,0:T(8,128)(2,1)}, bf16[128,2048]{1,0:T(8,128)(2,1)S(1)}, u32[]{:S(2)}, u32[]{:S(2)}) collective-permute-start(bf16[128,2048]{1,0:T(8,128)(2,1)} %bitcast.22), channel_id=1, source_target_pairs={{0,32},{32,64},{64,96},{96,128},{128,160},{160,192},{192,224},{1,3... | collective-permute-start | bytes 1572872 | tf_op jit(solution)/shard_map/ppermute | solution.py:234
  5.1 8.0 %collective-permute-start.2 = (bf16[128,2048]{1,0:T(8,128)(2,1)}, bf16[128,2048]{1,0:T(8,128)(2,1)S(1)}, u32[]{:S(2)}, u32[]{:S(2)}) collective-permute-start(bf16[128,2048]{1,0:T(8,128)(2,1)} %bitcast.23), channel_id=1, source_target_pairs={{0,36},{4,32},{64,100},{68,96},{128,164},{132,160},{192,228},{196,... | collective-permute-start | bytes 1572872 | tf_op jit(solution)/shard_map/ppermute | solution.py:257
  13.2 1.1 broadcast_select_fusion.1.g_ref
  14.3 1.3 broadcast_select_fusion.2.x_ref
  15.6 10.1 %collective-permute-done.2 = bf16[128,2048]{1,0:T(8,128)(2,1)S(1)} collective-permute-done((bf16[128,2048]{1,0:T(8,128)(2,1)}, bf16[128,2048]{1,0:T(8,128)(2,1)S(1)}, u32[]{:S(2)}, u32[]{:S(2)}) %collective-permute-start.2) | collective-permute-done | bytes 524320 | tf_op jit(solution)/shard_map/ppermute | solution.py:257
  25.7 5.3 %collective-permute-start.3 = (bf16[128,2048]{1,0:T(8,128)(2,1)S(1)}, bf16[128,2048]{1,0:T(8,128)(2,1)S(1)}, u32[]{:S(2)}, u32[]{:S(2)}) collective-permute-start(bf16[128,2048]{1,0:T(8,128)(2,1)S(1)} %broadcast_select_fusion.2.x_ref), channel_id=1, source_target_pairs={{0,4},{4,0},{1,5},{5,1},{2,6},{6,2},{3,7},{7,3},{8,12},{12,8},{9,1... | collective-permute-start | bytes 1572872 | tf_op jit(solution)/shard_map/ppermute | solution.py:239
  31.1 2.8 %pack.2 = bf16[16,48,2048]{2,1,0:T(8,128)(2,1)} custom-call(s32[1]{0:T(128)} %bitcast.half_ref, f32[8,128]{1,0:T(8,128)S(1)} %pad_maximum_fusion.meta_ref, s32[1,32]{1,0:T(1,128)S(1)} %copy-done.11, bf16[128,2048]{1,0:T(8,128)(2,1)S(1)} %broadcast_select_fusion.2.x_ref, bf16[128,2048]{1,0:T(8,128)(2,1)S(1)} %broadcast_select_fusion.1.g_ref), custom_call_target="tpu_custom_call" | custom-call | flops 402653184 | bytes 4194304 | tf_op jit(solution)/shard_map/pack/pallas_call | solution.py:83
  33.9 10.1 %collective-permute-done.3 = bf16[128,2048]{1,0:T(8,128)(2,1)S(1)} collective-permute-done((bf16[128,2048]{1,0:T(8,128)(2,1)S(1)}, bf16[128,2048]{1,0:T(8,128)(2,1)S(1)}, u32[]{:S(2)}, u32[]{:S(2)}) %collective-permute-start.3) | collective-permute-done | bytes 524320 | tf_op jit(solution)/shard_map/ppermute | solution.py:239
  44.1 7.5 %all-to-all-start = ((bf16[16,48,2048]{2,1,0:T(8,128)(2,1)}), bf16[16,48,2048]{2,1,0:T(8,128)(2,1)}, u32[]{:S(2)}, u32[]{:S(2)}) async-start(bf16[16,48,2048]{2,1,0:T(8,128)(2,1)} %pack.2), calls=%async_computation | async-start | bytes 6291456 | tf_op jit(solution)/shard_map/all_to_all | solution.py:243
  51.6 3.9 %collective-permute-start.5 = (bf16[128,2048]{1,0:T(8,128)(2,1)S(1)}, bf16[128,2048]{1,0:T(8,128)(2,1)S(1)}, u32[]{:S(2)}, u32[]{:S(2)}) collective-permute-start(bf16[128,2048]{1,0:T(8,128)(2,1)S(1)} %broadcast_select_fusion.1.g_ref), channel_id=1, source_target_pairs={{0,4},{4,0},{32,36},{36,32},{1,5},{5,1},{33,37},{37,33},{2,6},{6,2... | collective-permute-start | bytes 1572872 | tf_op jit(solution)/shard_map/ppermute | solution.py:239
  55.5 2.1 collective-permute-start.4
  57.6 11.3 %collective-permute-done.4.meta_ref = f32[8,128]{1,0:T(8,128)S(1)} collective-permute-done((f32[8,128]{1,0:T(8,128)S(1)}, f32[8,128]{1,0:T(8,128)S(1)}, u32[]{:S(2)}, u32[]{:S(2)}) %collective-permute-start.4) | collective-permute-done | bytes 4128 | tf_op jit(solution)/shard_map/ppermute | solution.py:239
  70.8 1.2 pack.3
  72.0 13.7 %all-to-all-done.in_ref = bf16[16,48,2048]{2,1,0:T(8,128)(2,1)} async-done(((bf16[16,48,2048]{2,1,0:T(8,128)(2,1)}), bf16[16,48,2048]{2,1,0:T(8,128)(2,1)}, u32[]{:S(2)}, u32[]{:S(2)}) %all-to-all-start) | async-done | bytes 3145760 | tf_op jit(solution)/shard_map/all_to_all | solution.py:243
  85.7 33.1 %all_to_all.20.in_ref = bf16[16,48,2048]{2,1,0:T(8,128)(2,1)S(1)} all-to-all(bf16[16,48,2048]{2,1,0:T(8,128)(2,1)S(1)} %pack.3), channel_id=1, replica_groups=mesh['z_lo'=4,'core'=2,'y'=4,'z_hi'=2,'x'=4] {'y','x'}, dimensions={0} | all-to-all | bytes 6291456 | tf_op jit(solution)/shard_map/all_to_all | solution.py:243
  118.7 11.7 %expert.3 = bf16[16,48,2048]{2,1,0:T(8,128)(2,1)S(1)} custom-call(bf16[16,48,2048]{2,1,0:T(8,128)(2,1)S(1)} %all_to_all.20.in_ref, bf16[2048,1536]{1,0:T(8,128)(2,1)} %bitcast.25, bf16[2048,1536]{1,0:T(8,128)(2,1)} %bitcast.26, bf16[768,2048]{1,0:T(8,128)(2,1)S(1)} %bitcast.19), custom_call_target="tpu_custom_call" | custom-call | flops 7247757312 | bytes 15728640 | tf_op jit(solution)/shard_map/expert/pallas_call | solution.py:204
  130.5 1.7 copy-done.5
  132.2 6.5 %all-to-all-start.2 = ((bf16[16,48,2048]{2,1,0:T(8,128)(2,1)}), bf16[16,48,2048]{2,1,0:T(8,128)(2,1)S(1)}, u32[]{:S(2)}, u32[]{:S(2)}) async-start(bf16[16,48,2048]{2,1,0:T(8,128)(2,1)} %copy-done.5), calls=%async_computation.2 | async-start | bytes 6291456 | tf_op jit(solution)/shard_map/all_to_all | solution.py:243
  138.7 1.9 copy-done.13
  140.6 12.7 %expert.2 = bf16[16,48,2048]{2,1,0:T(8,128)(2,1)S(1)} custom-call(bf16[16,48,2048]{2,1,0:T(8,128)(2,1)} %all-to-all-done.in_ref, bf16[2048,1536]{1,0:T(8,128)(2,1)} %bitcast.27, bf16[2048,1536]{1,0:T(8,128)(2,1)} %bitcast.28, bf16[768,2048]{1,0:T(8,128)(2,1)S(1)} %bitcast.20), custom_call_target="tpu_custom_call" | custom-call | flops 7247757312 | bytes 15728640 | tf_op jit(solution)/shard_map/expert/pallas_call | solution.py:204
  153.4 1.6 copy-done.4
  155.0 16.5 %all-to-all-done.2.rows_ref = bf16[16,48,2048]{2,1,0:T(8,128)(2,1)S(1)} async-done(((bf16[16,48,2048]{2,1,0:T(8,128)(2,1)}), bf16[16,48,2048]{2,1,0:T(8,128)(2,1)S(1)}, u32[]{:S(2)}, u32[]{:S(2)}) %all-to-all-start.2) | async-done | bytes 3145760 | tf_op jit(solution)/shard_map/all_to_all | solution.py:243
  171.4 1.7 copy-done
  173.1 7.9 %all-to-all-start.3 = ((bf16[16,48,2048]{2,1,0:T(8,128)(2,1)}), bf16[16,48,2048]{2,1,0:T(8,128)(2,1)S(1)}, u32[]{:S(2)}, u32[]{:S(2)}) async-start(bf16[16,48,2048]{2,1,0:T(8,128)(2,1)} %copy-done.4), calls=%async_computation.3 | async-start | bytes 6291456 | tf_op jit(solution)/shard_map/all_to_all | solution.py:243
  181.1 1.9 copy-done.1
  184.0 1.8 collect.1
  185.7 2.4 %collective-permute-start.6 = (bf16[272,2048]{1,0:T(8,128)(2,1)S(1)}, bf16[272,2048]{1,0:T(8,128)(2,1)S(1)}, u32[]{:S(2)}, u32[]{:S(2)}) collective-permute-start(bf16[272,2048]{1,0:T(8,128)(2,1)S(1)} %collect.1), channel_id=1, source_target_pairs={{0,4},{4,0},{32,36},{36,32},{1,5},{5,1},{33,37},{37,33},{2,6},{6,2... | collective-permute-start | bytes 3342344 | tf_op jit(solution)/shard_map/ppermute | solution.py:239
  188.1 35.8 %collective-permute-done.6.refs_0_ = bf16[272,2048]{1,0:T(8,128)(2,1)S(1)} collective-permute-done((bf16[272,2048]{1,0:T(8,128)(2,1)S(1)}, bf16[272,2048]{1,0:T(8,128)(2,1)S(1)}, u32[]{:S(2)}, u32[]{:S(2)}) %collective-permute-start.6) | collective-permute-done | bytes 1114144 | tf_op jit(solution)/shard_map/ppermute | solution.py:239
  224.9 1.0 copy-done.3
  226.0 1.2 copy-done.10
  227.2 2.5 %collect_last.1 = (bf16[128,2048]{1,0:T(8,128)(2,1)}, bf16[128,2048]{1,0:T(8,128)(2,1)}, f32[4,128]{1,0:T(4,128)}) custom-call(s32[1]{0:T(128)} %bitcast.half_ref, f32[8,128]{1,0:T(8,128)S(1)} %pad_maximum_fusion.meta_ref, s32[1,32]{1,0:T(1,128)S(1)} %copy-done.11, bf16[16,48,2048]{2,1,0:T(8,128)(2,1)S(1)} %all-to-all-done.3.rows_ref, ...), custom_call_target="tpu_custom_call" | custom-call | flops 805306368 | bytes 5242880 | tf_op jit(solution)/shard_map/collect_last/pallas_call | solution.py:146
  (32 shorter events, 4.0 us)
Async XLA Ops:
  0.6 30.4 %copy-start.14 = (s32[1,128,4]{1,2,0:T(4,128)S(1)}, s32[1,128,4]{1,2,0:T(4,128)}, u32[]{:S(2)}) copy-start(s32[1,128,4]{1,2,0:T(4,128)} %param.9) | copy-start | bytes 6148
  0.6 30.4 %copy-start.15 = (f32[1,128,4]{1,2,0:T(4,128)S(1)}, f32[1,128,4]{1,2,0:T(4,128)}, u32[]{:S(2)}) copy-start(f32[1,128,4]{1,2,0:T(4,128)} %param.10) | copy-start | bytes 6148
  0.7 30.4 %copy-start.11 = (s32[1,32]{1,0:T(1,128)S(1)}, s32[1,32]{1,0:T(1,128)}, u32[]{:S(2)}) copy-start(s32[1,32]{1,0:T(1,128)} %table_ref.7) | copy-start | bytes 388
  0.7 12.5 %collective-permute-start.1 = (bf16[128,2048]{1,0:T(8,128)(2,1)}, bf16[128,2048]{1,0:T(8,128)(2,1)S(1)}, u32[]{:S(2)}, u32[]{:S(2)}) collective-permute-start(bf16[128,2048]{1,0:T(8,128)(2,1)} %bitcast.21), channel_id=1, source_target_pairs={{32,0},{64,32},{96,64},{128,96},{160,128},{192,160},{224,192},{33,... | collective-permute-start | bytes 1572872 | tf_op jit(solution)/shard_map/ppermute | solution.py:234
  2.7 11.6 %collective-permute-start = (bf16[128,2048]{1,0:T(8,128)(2,1)}, bf16[128,2048]{1,0:T(8,128)(2,1)S(1)}, u32[]{:S(2)}, u32[]{:S(2)}) collective-permute-start(bf16[128,2048]{1,0:T(8,128)(2,1)} %bitcast.22), channel_id=1, source_target_pairs={{0,32},{32,64},{64,96},{96,128},{128,160},{160,192},{192,224},{1,3... | collective-permute-start | bytes 1572872 | tf_op jit(solution)/shard_map/ppermute | solution.py:234
  5.1 20.6 %collective-permute-start.2 = (bf16[128,2048]{1,0:T(8,128)(2,1)}, bf16[128,2048]{1,0:T(8,128)(2,1)S(1)}, u32[]{:S(2)}, u32[]{:S(2)}) collective-permute-start(bf16[128,2048]{1,0:T(8,128)(2,1)} %bitcast.23), channel_id=1, source_target_pairs={{0,36},{4,32},{64,100},{68,96},{128,164},{132,160},{192,228},{196,... | collective-permute-start | bytes 1572872 | tf_op jit(solution)/shard_map/ppermute | solution.py:257
  14.3 37.3 %copy-start.2 = (bf16[128,2048]{1,0:T(8,128)(2,1)}, bf16[128,2048]{1,0:T(8,128)(2,1)S(1)}, u32[]{:S(2)}) copy-start(bf16[128,2048]{1,0:T(8,128)(2,1)S(1)} %broadcast_select_fusion.1.g_ref) | copy-start | bytes 1572868
  25.7 18.3 %collective-permute-start.3 = (bf16[128,2048]{1,0:T(8,128)(2,1)S(1)}, bf16[128,2048]{1,0:T(8,128)(2,1)S(1)}, u32[]{:S(2)}, u32[]{:S(2)}) collective-permute-start(bf16[128,2048]{1,0:T(8,128)(2,1)S(1)} %broadcast_select_fusion.2.x_ref), channel_id=1, source_target_pairs={{0,4},{4,0},{1,5},{5,1},{2,6},{6,2},{3,7},{7,3},{8,12},{12,8},{9,1... | collective-permute-start | bytes 1572872 | tf_op jit(solution)/shard_map/ppermute | solution.py:239
  44.1 41.6 %all-to-all-start = ((bf16[16,48,2048]{2,1,0:T(8,128)(2,1)}), bf16[16,48,2048]{2,1,0:T(8,128)(2,1)}, u32[]{:S(2)}, u32[]{:S(2)}) async-start(bf16[16,48,2048]{2,1,0:T(8,128)(2,1)} %pack.2), calls=%async_computation | async-start | bytes 6291456 | tf_op jit(solution)/shard_map/all_to_all | solution.py:243
  51.6 17.4 %collective-permute-start.5 = (bf16[128,2048]{1,0:T(8,128)(2,1)S(1)}, bf16[128,2048]{1,0:T(8,128)(2,1)S(1)}, u32[]{:S(2)}, u32[]{:S(2)}) collective-permute-start(bf16[128,2048]{1,0:T(8,128)(2,1)S(1)} %broadcast_select_fusion.1.g_ref), channel_id=1, source_target_pairs={{0,4},{4,0},{32,36},{36,32},{1,5},{5,1},{33,37},{37,33},{2,6},{6,2... | collective-permute-start | bytes 1572872 | tf_op jit(solution)/shard_map/ppermute | solution.py:239
  55.5 13.5 %collective-permute-start.4 = (f32[8,128]{1,0:T(8,128)S(1)}, f32[8,128]{1,0:T(8,128)S(1)}, u32[]{:S(2)}, u32[]{:S(2)}) collective-permute-start(f32[8,128]{1,0:T(8,128)S(1)} %pad_maximum_fusion.meta_ref), channel_id=1, source_target_pairs={{0,4},{4,0},{32,36},{36,32},{1,5},{5,1},{33,37},{37,33},{2,6},{6,2... | collective-permute-start | bytes 12296 | tf_op jit(solution)/shard_map/ppermute | solution.py:239
  69.0 0.8 copy-start.6
  69.8 1.0 copy-start.7
  85.7 33.1 %copy-start.12 = (bf16[1,1,768,2048]{3,2,1,0:T(8,128)(2,1)S(1)}, bf16[1,1,768,2048]{3,2,1,0:T(8,128)(2,1)}, u32[]{:S(2)}) copy-start(bf16[1,1,768,2048]{3,2,1,0:T(8,128)(2,1)} %param.13) | copy-start | bytes 9437188
  130.5 1.7 copy-start.5
  132.2 39.3 %all-to-all-start.2 = ((bf16[16,48,2048]{2,1,0:T(8,128)(2,1)}), bf16[16,48,2048]{2,1,0:T(8,128)(2,1)S(1)}, u32[]{:S(2)}, u32[]{:S(2)}) async-start(bf16[16,48,2048]{2,1,0:T(8,128)(2,1)} %copy-done.5), calls=%async_computation.2 | async-start | bytes 6291456 | tf_op jit(solution)/shard_map/all_to_all | solution.py:243
  138.7 1.9 copy-start.13
  153.3 1.6 copy-start.4
  171.4 1.7 copy-start
  173.1 51.8 %all-to-all-start.3 = ((bf16[16,48,2048]{2,1,0:T(8,128)(2,1)}), bf16[16,48,2048]{2,1,0:T(8,128)(2,1)S(1)}, u32[]{:S(2)}, u32[]{:S(2)}) async-start(bf16[16,48,2048]{2,1,0:T(8,128)(2,1)} %copy-done.4), calls=%async_computation.3 | async-start | bytes 6291456 | tf_op jit(solution)/shard_map/all_to_all | solution.py:243
  181.1 1.9 copy-start.1
  182.9 1.0 copy-start.8
  185.7 38.2 %collective-permute-start.6 = (bf16[272,2048]{1,0:T(8,128)(2,1)S(1)}, bf16[272,2048]{1,0:T(8,128)(2,1)S(1)}, u32[]{:S(2)}, u32[]{:S(2)}) collective-permute-start(bf16[272,2048]{1,0:T(8,128)(2,1)S(1)} %collect.1), channel_id=1, source_target_pairs={{0,4},{4,0},{32,36},{36,32},{1,5},{5,1},{33,37},{37,33},{2,6},{6,2... | collective-permute-start | bytes 3342344 | tf_op jit(solution)/shard_map/ppermute | solution.py:239
  223.9 1.0 copy-start.9
  224.9 1.0 copy-start.3
  226.0 1.2 copy-start.10
